TPU v7x, 32 devices: a whole 2x2x4 slice. The times are simulated.
32 devices in a mesh: groups: 2 (over x), blk: 16 (over z, y, core).
Axes of the slice: x: 2, y: 2, z: 4, core: 2. Of those that a mesh axis runs over, the one named last changes fastest.
Arguments:
- query: bfloat16 [8192, 1024], P(('groups', 'blk')), parts along dimension 0, may hold values from -5 to 5
- key_in: bfloat16 [8192, 1024], P(('groups', 'blk')), parts along dimension 0, may hold values from -6 to 6
- value: bfloat16 [8192, 1024], P(('groups', 'blk')), parts along dimension 0, may hold values from -6 to 6
- grad_out: bfloat16 [8192, 1024], P(('groups', 'blk')), parts along dimension 0, may hold values from -6 to 6
- neighbors: int32 [64, 8], P(('groups', 'blk')), parts along dimension 0, may hold values from 0 to 31, as said below
- counts: int32 [64], P(('groups', 'blk')), parts along dimension 0, may hold values from 2 to 8, as said below
Outputs:
- attn_out: bfloat16 [8192, 1024], P(('groups', 'blk')), parts along dimension 0
- grad_query: bfloat16 [8192, 1024], P(('groups', 'blk')), parts along dimension 0
- grad_key: bfloat16 [8192, 1024], P(('groups', 'blk')), parts along dimension 0
- grad_value: bfloat16 [8192, 1024], P(('groups', 'blk')), parts along dimension 0
There are 2 independent parts, one for each index of `groups`. A program takes and returns all parts, laid end to end along the dimension named above; each array names one. Nothing has to cross between parts.
Inputs may be any that keep to these rules, and one draw needn't show every extreme that they name: `neighbors`: row b holds 8 distinct block indices; its first entry is b itself; every entry is a block whose device (block // 2) is at most 2 steps from b's device along blk, counted cyclically; only the first counts[b] entries are used. `counts`: some block has exactly 8 and some exactly 2.
All inputs are finite; a program needn't handle non-finite values.
Results may differ from a plain program's by a relative error of at most 0.0086.
Values may be sent and summed in bfloat16 or wider, within the bound.
A program may use at most 128 MiB of HBM per device.

v0:
```python
import math

import jax
import jax.numpy as jnp
from jax import lax
from jax.sharding import PartitionSpec as P

HEADS = 16
REACH = 2


def shifted(x, axis, by):
    length = lax.axis_size(axis)
    return lax.ppermute(x, axis, [(i, (i + by) % length) for i in range(length)])


def split_heads(matrix):
    return matrix.reshape(matrix.shape[0], HEADS, matrix.shape[1] // HEADS)


def merge_heads(matrix):
    return matrix.reshape(matrix.shape[0], matrix.shape[1] * matrix.shape[2])


def block_slice(matrix, blk_id, blk_len):
    return lax.dynamic_slice_in_dim(matrix, blk_id * blk_len, blk_len, 0)


def local(query, key_in, value, grad_out, neighbors, counts):
    row_count, model_width = query.shape
    own_blocks = neighbors.shape[0]
    list_width = neighbors.shape[1]
    blk_len = row_count // own_blocks
    head_dim = model_width // HEADS
    factor = 1.0 / math.sqrt(head_dim)
    shard_count = lax.axis_size("blk")
    shard_index = lax.axis_index("blk")
    span_blocks = (2 * REACH + 1) * own_blocks
    paired = jnp.stack([key_in, value])
    pieces = {0: paired}
    for direction in (1, -1):
        current = paired
        for distance in range(1, REACH + 1):
            current = shifted(current, "blk", -direction)
            pieces[direction * distance] = current
    window = jnp.concatenate([pieces[offset] for offset in range(-REACH, REACH + 1)], axis=1)
    window_tiles = window.reshape(2, span_blocks, blk_len, model_width)
    shard_pos = jnp.mod(neighbors // own_blocks - shard_index + REACH, shard_count)
    slot_table = shard_pos * own_blocks + neighbors % own_blocks
    slot_ids = jnp.arange(list_width, dtype=jnp.int32)

    def block_inputs(blk_id):
        slots = slot_table[blk_id]
        picked = window_tiles[:, slots]
        k_all = split_heads(picked[0].reshape(list_width * blk_len, model_width))
        v_all = split_heads(picked[1].reshape(list_width * blk_len, model_width))
        live_keys = jnp.repeat(slot_ids < counts[blk_id], blk_len)
        q_tile = split_heads(block_slice(query, blk_id, blk_len))
        scores = (
            jnp.einsum("qhd,khd->hqk", q_tile, k_all, preferred_element_type=jnp.float32) * factor
        )
        scores = jnp.where(live_keys[None, None, :], scores, -jnp.inf)
        return (slots, q_tile, k_all, v_all, scores)

    def forward_block(blk_id):
        slots, q_tile, k_all, v_all, scores = block_inputs(blk_id)
        row_top = jnp.max(scores, axis=2)
        exponent = jnp.exp(scores - row_top[:, :, None])
        row_sum = jnp.sum(exponent, axis=2)
        rounded = (exponent / row_sum[:, :, None]).astype(jnp.bfloat16)
        mixed = jnp.einsum("hqk,khd->qhd", rounded, v_all, preferred_element_type=jnp.float32)
        return (merge_heads(mixed).astype(jnp.bfloat16), row_top, row_sum)

    out_blocks, row_tops, row_sums = lax.map(forward_block, jnp.arange(own_blocks, dtype=jnp.int32))
    attn_out = out_blocks.reshape(row_count, model_width)
    row_delta = jnp.sum(
        split_heads(grad_out).astype(jnp.float32) * split_heads(attn_out).astype(jnp.float32),
        axis=2,
    )

    def query_pass(grad_window):

        def outer_step(grad_win, blk_id):
            slots, q_tile, k_all, v_all, scores = block_inputs(blk_id)
            g_tile = split_heads(block_slice(grad_out, blk_id, blk_len))
            delta_tile = block_slice(row_delta, blk_id, blk_len).T
            soft_probs = (
                jnp.exp(scores - row_tops[blk_id][:, :, None]) / row_sums[blk_id][:, :, None]
            )
            dprobs = jnp.einsum("qhd,khd->hqk", g_tile, v_all, preferred_element_type=jnp.float32)
            dscores = (soft_probs * (dprobs - delta_tile[:, :, None])).astype(jnp.bfloat16)
            grad_q = (
                jnp.einsum("hqk,khd->qhd", dscores, k_all, preferred_element_type=jnp.float32)
                * factor
            )
            probs_rounded = soft_probs.astype(jnp.bfloat16)
            dk_all = (
                jnp.einsum("hqk,qhd->khd", dscores, q_tile, preferred_element_type=jnp.float32)
                * factor
            )
            dv_all = jnp.einsum(
                "hqk,qhd->khd", probs_rounded, g_tile, preferred_element_type=jnp.float32
            )
            grad_win = grad_win.at[0, slots].add(dk_all.reshape(list_width, blk_len, model_width))
            grad_win = grad_win.at[1, slots].add(dv_all.reshape(list_width, blk_len, model_width))
            return (grad_win, merge_heads(grad_q))

        grad_win, grad_blocks = lax.scan(
            outer_step, grad_window, jnp.arange(own_blocks, dtype=jnp.int32)
        )
        return (grad_blocks.reshape(row_count, model_width), grad_win)

    grad_all, grad_tiles = query_pass(
        jnp.zeros((2, span_blocks, blk_len, model_width), jnp.float32)
    )
    grad_win = grad_tiles.reshape(2, span_blocks * blk_len, model_width)

    def window_piece(offset):
        return lax.slice_in_dim(
            grad_win, (offset + REACH) * row_count, (offset + REACH + 1) * row_count, axis=1
        )

    summed = window_piece(0)
    for direction in (1, -1):
        carried = window_piece(direction * REACH)
        for distance in range(REACH - 1, -1, -1):
            carried = shifted(carried.astype(jnp.bfloat16), "blk", direction).astype(carried.dtype)
            if distance > 0:
                carried = carried + window_piece(direction * distance)
        summed = summed + carried
    grad_key = summed[0].astype(jnp.bfloat16)
    grad_value = summed[1].astype(jnp.bfloat16)
    grad_query = grad_all.astype(jnp.bfloat16)
    return (attn_out, grad_query, grad_key, grad_value)


def solution(mesh):
    in_specs = (
        P(("groups", "blk"), None),
        P(("groups", "blk"), None),
        P(("groups", "blk"), None),
        P(("groups", "blk"), None),
        P(("groups", "blk"), None),
        P(("groups", "blk")),
    )
    out_specs = (
        P(("groups", "blk"), None),
        P(("groups", "blk"), None),
        P(("groups", "blk"), None),
        P(("groups", "blk"), None),
    )
    return jax.shard_map(local, mesh=mesh, in_specs=in_specs, out_specs=out_specs, check_vma=False)
```

profile of v0, /device:TPU:1, one launch (start us, length us, event | category | flops | bytes accessed | tf_op | source)
XLA Modules:
  0.0 352.6 jit_solution(11672745346984228568)
XLA Ops:
  4.7 23.0 %collective-permute-done = bf16[2,256,1024]{2,1,0:T(8,128)(2,1)} collective-permute-done((bf16[2,256,1024]{2,1,0:T(8,128)(2,1)S(1)}, bf16[2,256,1024]{2,1,0:T(8,128)(2,1)}, u32[]{:S(2)}, u32[]{:S(2)}) %collective-permute-start) | collective-permute-done | bytes 1048608 | tf_op jit(solution)/shard_map/ppermute | solution.py:14
  30.3 11.1 %collective-permute-done.2 = bf16[2,256,1024]{2,1,0:T(8,128)(2,1)S(1)} collective-permute-done((bf16[2,256,1024]{2,1,0:T(8,128)(2,1)S(1)}, bf16[2,256,1024]{2,1,0:T(8,128)(2,1)S(1)}, u32[]{:S(2)}, u32[]{:S(2)}) %collective-permute-start.2) | collective-permute-done | bytes 1048608 | tf_op jit(solution)/shard_map/ppermute | solution.py:14
  44.7 7.8 %collective-permute-done.1 = bf16[2,256,1024]{2,1,0:T(8,128)(2,1)} collective-permute-done((bf16[2,256,1024]{2,1,0:T(8,128)(2,1)}, bf16[2,256,1024]{2,1,0:T(8,128)(2,1)}, u32[]{:S(2)}, u32[]{:S(2)}) %collective-permute-start.1) | collective-permute-done | bytes 1048608 | tf_op jit(solution)/shard_map/ppermute | solution.py:14
  59.4 69.0 %while.28 = (s32[]{:T(128)}, bf16[2,128,1024]{1,2,0:T(8,128)(2,1)}, f32[2,16,128]{2,1,0:T(8,128)S(1)}, f32[2,16,128]{2,1,0:T(8,128)S(1)}, s32[2]{0:T(128)S(1)}, ...) while((s32[]{:T(128)}, bf16[2,128,1024]{1,2,0:T(8,128)(2,1)}, ...), condition=%wide.region_3.4_spmd.clone, body=%wide.region_0.3_spmd.clone.sunk | while | flops 562164736 | bytes 77152744 | solution.py:74
  64.3 5.3 %gather_fusion = bf16[8,2,128,1024]{3,2,1,0:T(8,128)(2,1)} fusion(bf16[2,10,128,1024]{3,2,1,0:T(8,128)(2,1)} %get-tuple-element.471, s32[1024]{0:T(1024)S(1)} %pad_clamp_fusion.4), kind=kCustom, calls=%fused_computation.clone.clone.1 | custom fusion | bytes 8388640 | tf_op jit(solution)/shard_map/while/body/eval_jaxpr/gather | solution.py:54
  69.6 4.8 %fusion.62 = (bf16[1,8,128,1024]{3,2,0,1:T(8,128)(2,1)}, bf16[1,8,128,1024]{3,2,0,1:T(8,128)(2,1)}) fusion(bf16[2,8,128,1024]{3,2,0,1:T(8,128)(2,1)} %bitcast.180), kind=kLoop, calls=%fused_computation.77.clone.1 | loop fusion | bytes 8388608 | tf_op jit(solution)/shard_map/while/body/eval_jaxpr/slice | solution.py:55
  98.8 5.3 %gather_fusion = bf16[8,2,128,1024]{3,2,1,0:T(8,128)(2,1)} fusion(bf16[2,10,128,1024]{3,2,1,0:T(8,128)(2,1)} %get-tuple-element.471, s32[1024]{0:T(1024)S(1)} %pad_clamp_fusion.4), kind=kCustom, calls=%fused_computation.clone.clone.1 | custom fusion | bytes 8388640 | tf_op jit(solution)/shard_map/while/body/eval_jaxpr/gather | solution.py:54
  104.1 4.8 %fusion.62 = (bf16[1,8,128,1024]{3,2,0,1:T(8,128)(2,1)}, bf16[1,8,128,1024]{3,2,0,1:T(8,128)(2,1)}) fusion(bf16[2,8,128,1024]{3,2,0,1:T(8,128)(2,1)} %bitcast.180), kind=kLoop, calls=%fused_computation.77.clone.1 | loop fusion | bytes 8388608 | tf_op jit(solution)/shard_map/while/body/eval_jaxpr/slice | solution.py:55
  132.1 5.3 %broadcast_in_dim.60 = f32[2,10,128,1024]{3,2,1,0:T(8,128)} broadcast(f32[]{:T(128)} %constant.94.clone.1), dimensions={} | broadcast | bytes 10485764 | tf_op jit(solution)/shard_map/broadcast_in_dim | solution.py:114
  137.4 153.3 %while.29 = (s32[]{:T(128)}, f32[2,10,128,1024]{3,2,1,0:T(8,128)}, bf16[2,128,1024]{1,2,0:T(8,128)(2,1)}, s32[2]{0:T(128)S(1)}, s32[2,8]{1,0:T(2,128)S(1)}, /*in...) while((s32[]{:T(128)}, f32[2,10,128,1024]{3,2,1,0:T(8,128)}, ...), condition=%wide.region_8.9_spmd.clone, body=%wide.region_5.8_spmd.clone.sunk | while | flops 1362363520 | bytes 160250608 | solution.py:108
  143.0 5.3 %gather_fusion.1 = bf16[8,2,128,1024]{3,2,1,0:T(8,128)(2,1)} fusion(bf16[2,10,128,1024]{3,2,1,0:T(8,128)(2,1)} %get-tuple-element.520, s32[1024]{0:T(1024)S(1)} %pad_clamp_fusion.5), kind=kCustom, calls=%fused_computation.1.clone.clone.1 | custom fusion | bytes 8388640 | tf_op jit(solution)/shard_map/while/body/eval_jaxpr/gather | solution.py:54
  178.9 5.4 %copy.49 = f32[8,128,1024]{2,1,0:T(8,128)} copy(f32[8,128,1024]{1,0,2:T(8,128)} %bitcast.183) | data formatting | bytes 8388608 | tf_op jit(solution)/shard_map/while/body/eval_jaxpr/reshape | solution.py:104
  184.4 5.3 %copy.50 = f32[128,8,8,128]{3,2,1,0:T(8,128)} copy(f32[128,8,8,128]{3,1,2,0:T(8,128)} %bitcast.179) | data formatting | bytes 8388608 | tf_op jit(solution)/shard_map/while
  189.6 5.5 %copy.51 = f32[8,128,1024]{2,1,0:T(8,128)} copy(f32[8,128,1024]{1,0,2:T(8,128)} %bitcast.184) | data formatting | bytes 8388608 | tf_op jit(solution)/shard_map/while/body/eval_jaxpr/reshape | solution.py:105
  195.2 9.4 %scatter_fusion = f32[2,10,128,1024]{3,2,1,0:T(8,128)} fusion(f32[2,10,128,1024]{3,2,1,0:T(8,128)} %get-tuple-element.497, s32[8]{0:T(128)S(1)} %select_bitcast_fusion.5, f32[8,128,1024]{2,1,0:T(8,128)} %copy.49), kind=kCustom, calls=%fused_computation.2.clone.clone.1 | custom fusion | flops 1048576 | bytes 12582976 | tf_op jit(solution)/shard_map/while/body/eval_jaxpr/scatter-add | solution.py:104
  204.6 9.5 %scatter_fusion.1 = f32[2,10,128,1024]{3,2,1,0:T(8,128)} fusion(f32[2,10,128,1024]{3,2,1,0:T(8,128)} %scatter_fusion, s32[8]{0:T(128)S(1)} %get-tuple-element.436, f32[8,128,1024]{2,1,0:T(8,128)} %copy.51), kind=kCustom, calls=%fused_computation.3.clone.clone.1 | custom fusion | flops 1048576 | bytes 12582976 | tf_op jit(solution)/shard_map/while/body/eval_jaxpr/scatter-add | solution.py:105
  219.6 5.3 %gather_fusion.1 = bf16[8,2,128,1024]{3,2,1,0:T(8,128)(2,1)} fusion(bf16[2,10,128,1024]{3,2,1,0:T(8,128)(2,1)} %get-tuple-element.520, s32[1024]{0:T(1024)S(1)} %pad_clamp_fusion.5), kind=kCustom, calls=%fused_computation.1.clone.clone.1 | custom fusion | bytes 8388640 | tf_op jit(solution)/shard_map/while/body/eval_jaxpr/gather | solution.py:54
  255.6 5.4 %copy.49 = f32[8,128,1024]{2,1,0:T(8,128)} copy(f32[8,128,1024]{1,0,2:T(8,128)} %bitcast.183) | data formatting | bytes 8388608 | tf_op jit(solution)/shard_map/while/body/eval_jaxpr/reshape | solution.py:104
  261.0 5.3 %copy.50 = f32[128,8,8,128]{3,2,1,0:T(8,128)} copy(f32[128,8,8,128]{3,1,2,0:T(8,128)} %bitcast.179) | data formatting | bytes 8388608 | tf_op jit(solution)/shard_map/while
  266.3 5.5 %copy.51 = f32[8,128,1024]{2,1,0:T(8,128)} copy(f32[8,128,1024]{1,0,2:T(8,128)} %bitcast.184) | data formatting | bytes 8388608 | tf_op jit(solution)/shard_map/while/body/eval_jaxpr/reshape | solution.py:105
  271.8 9.4 %scatter_fusion = f32[2,10,128,1024]{3,2,1,0:T(8,128)} fusion(f32[2,10,128,1024]{3,2,1,0:T(8,128)} %get-tuple-element.497, s32[8]{0:T(128)S(1)} %select_bitcast_fusion.5, f32[8,128,1024]{2,1,0:T(8,128)} %copy.49), kind=kCustom, calls=%fused_computation.2.clone.clone.1 | custom fusion | flops 1048576 | bytes 12582976 | tf_op jit(solution)/shard_map/while/body/eval_jaxpr/scatter-add | solution.py:104
  281.3 9.5 %scatter_fusion.1 = f32[2,10,128,1024]{3,2,1,0:T(8,128)} fusion(f32[2,10,128,1024]{3,2,1,0:T(8,128)} %scatter_fusion, s32[8]{0:T(128)S(1)} %get-tuple-element.436, f32[8,128,1024]{2,1,0:T(8,128)} %copy.51), kind=kCustom, calls=%fused_computation.3.clone.clone.1 | custom fusion | flops 1048576 | bytes 12582976 | tf_op jit(solution)/shard_map/while/body/eval_jaxpr/scatter-add | solution.py:105
  297.7 22.3 %collective-permute-done.4 = bf16[2,256,1024]{2,1,0:T(8,128)(2,1)S(1)} collective-permute-done((bf16[2,256,1024]{2,1,0:T(8,128)(2,1)S(1)}, bf16[2,256,1024]{2,1,0:T(8,128)(2,1)S(1)}, u32[]{:S(2)}, u32[]{:S(2)}) %collective-permute-start.4) | collective-permute-done | bytes 1048608 | tf_op jit(solution)/shard_map/ppermute | solution.py:14
  329.0 20.5 %collective-permute-done.5 = bf16[2,256,1024]{2,1,0:T(8,128)(2,1)S(1)} collective-permute-done((bf16[2,256,1024]{2,1,0:T(8,128)(2,1)}, bf16[2,256,1024]{2,1,0:T(8,128)(2,1)S(1)}, u32[]{:S(2)}, u32[]{:S(2)}) %collective-permute-start.5) | collective-permute-done | bytes 1048608 | tf_op jit(solution)/shard_map/ppermute | solution.py:14
  (150 shorter events, 149.9 us)
Async XLA Ops:
  0.6 44.1 %copy-start.11 = (s32[2,8]{1,0:T(2,128)S(1)}, s32[2,8]{1,0:T(2,128)}, u32[]{:S(2)}) copy-start(s32[2,8]{1,0:T(2,128)} %param.14) | copy-start | bytes 196
  0.6 54.5 %copy-start.6 = (bf16[256,1024]{1,0:T(8,128)(2,1)S(1)}, bf16[256,1024]{1,0:T(8,128)(2,1)}, u32[]{:S(2)}) copy-start(bf16[256,1024]{1,0:T(8,128)(2,1)} %param.12) | copy-start | bytes 1572868
  0.7 54.5 %copy-start.7 = (bf16[256,1024]{1,0:T(8,128)(2,1)S(1)}, bf16[256,1024]{1,0:T(8,128)(2,1)}, u32[]{:S(2)}) copy-start(bf16[256,1024]{1,0:T(8,128)(2,1)} %param.11) | copy-start | bytes 1572868
  2.0 25.7 %collective-permute-start = (bf16[2,256,1024]{2,1,0:T(8,128)(2,1)S(1)}, bf16[2,256,1024]{2,1,0:T(8,128)(2,1)}, u32[]{:S(2)}, u32[]{:S(2)}) collective-permute-start(bf16[2,256,1024]{2,1,0:T(8,128)(2,1)S(1)} %pad_maximum_fusion), channel_id=1, source_target_pairs={{0,1},{1,2},{2,3},{3,4},{4,5},{5,6},{6,7},{7,8},{8,9},{9,10},{10,1... | collective-permute-start | bytes 3145736 | tf_op jit(solution)/shard_map/ppermute | solution.py:14
  4.7 36.7 %collective-permute-start.2 = (bf16[2,256,1024]{2,1,0:T(8,128)(2,1)S(1)}, bf16[2,256,1024]{2,1,0:T(8,128)(2,1)S(1)}, u32[]{:S(2)}, u32[]{:S(2)}) collective-permute-start(bf16[2,256,1024]{2,1,0:T(8,128)(2,1)S(1)} %pad_maximum_fusion), channel_id=1, source_target_pairs={{0,15},{1,0},{2,1},{3,2},{4,3},{5,4},{6,5},{7,6},{8,7},{9,8},{10,9... | collective-permute-start | bytes 3145736 | tf_op jit(solution)/shard_map/ppermute | solution.py:14
  27.7 24.8 %collective-permute-start.1 = (bf16[2,256,1024]{2,1,0:T(8,128)(2,1)}, bf16[2,256,1024]{2,1,0:T(8,128)(2,1)}, u32[]{:S(2)}, u32[]{:S(2)}) collective-permute-start(bf16[2,256,1024]{2,1,0:T(8,128)(2,1)} %collective-permute-done), channel_id=1, source_target_pairs={{0,1},{1,2},{2,3},{3,4},{4,5},{5,6},{6,7},{7,8},{8,9},{9,10},{10,1... | collective-permute-start | bytes 3145736 | tf_op jit(solution)/shard_map/ppermute | solution.py:14
  41.4 14.3 %collective-permute-start.3 = (bf16[2,256,1024]{2,1,0:T(8,128)(2,1)S(1)}, bf16[2,256,1024]{2,1,0:T(8,128)(2,1)}, u32[]{:S(2)}, u32[]{:S(2)}) collective-permute-start(bf16[2,256,1024]{2,1,0:T(8,128)(2,1)S(1)} %collective-permute-done.2), channel_id=1, source_target_pairs={{0,15},{1,0},{2,1},{3,2},{4,3},{5,4},{6,5},{7,6},{8,7},{9,8},{10,9... | collective-permute-start | bytes 3145736 | tf_op jit(solution)/shard_map/ppermute | solution.py:14
  53.8 5.6 %copy-start.12 = (s32[2]{0:T(128)S(1)}, s32[2]{0:T(128)}, u32[]{:S(2)}) copy-start(s32[2]{0:T(128)} %param.15) | copy-start | bytes 28
  57.1 2.4 copy-start
  88.5 2.0 copy-start.2
  90.5 2.6 copy-start.3
  125.0 2.6 copy-start.3
  166.6 2.6 copy-start.1
  189.6 5.5 %copy-start.8 = (bf16[2,128,1024]{1,2,0:T(8,128)(2,1)S(1)}, bf16[2,128,1024]{1,2,0:T(8,128)(2,1)}, u32[]{:S(2)}) copy-start(bf16[2,128,1024]{1,2,0:T(8,128)(2,1)} %get-tuple-element.498) | copy-start | bytes 1572868 | tf_op jit(solution)/shard_map/while
  195.1 9.4 %copy-start.9 = (bf16[2,128,1024]{1,2,0:T(8,128)(2,1)}, bf16[2,128,1024]{1,2,0:T(8,128)(2,1)S(1)}, u32[]{:S(2)}) copy-start(bf16[2,128,1024]{1,2,0:T(8,128)(2,1)S(1)} %constant_dynamic-update-slice_fusion.10) | copy-start | bytes 1572868 | tf_op jit(solution)/shard_map/while
  243.2 2.6 copy-start.1
  266.3 5.5 %copy-start.8 = (bf16[2,128,1024]{1,2,0:T(8,128)(2,1)S(1)}, bf16[2,128,1024]{1,2,0:T(8,128)(2,1)}, u32[]{:S(2)}) copy-start(bf16[2,128,1024]{1,2,0:T(8,128)(2,1)} %get-tuple-element.498) | copy-start | bytes 1572868 | tf_op jit(solution)/shard_map/while
  271.8 9.5 %copy-start.9 = (bf16[2,128,1024]{1,2,0:T(8,128)(2,1)}, bf16[2,128,1024]{1,2,0:T(8,128)(2,1)S(1)}, u32[]{:S(2)}) copy-start(bf16[2,128,1024]{1,2,0:T(8,128)(2,1)S(1)} %constant_dynamic-update-slice_fusion.10) | copy-start | bytes 1572868 | tf_op jit(solution)/shard_map/while
  295.7 24.3 %collective-permute-start.4 = (bf16[2,256,1024]{2,1,0:T(8,128)(2,1)S(1)}, bf16[2,256,1024]{2,1,0:T(8,128)(2,1)S(1)}, u32[]{:S(2)}, u32[]{:S(2)}) collective-permute-start(bf16[2,256,1024]{2,1,0:T(8,128)(2,1)S(1)} %get-tuple-element.277), channel_id=1, source_target_pairs={{0,1},{1,2},{2,3},{3,4},{4,5},{5,6},{6,7},{7,8},{8,9},{9,10},{10,1... | collective-permute-start | bytes 3145736 | tf_op jit(solution)/shard_map/ppermute | solution.py:14
  297.7 22.3 %collective-permute-start.6 = (bf16[2,256,1024]{2,1,0:T(8,128)(2,1)S(1)}, bf16[2,256,1024]{2,1,0:T(8,128)(2,1)S(1)}, u32[]{:S(2)}, u32[]{:S(2)}) collective-permute-start(bf16[2,256,1024]{2,1,0:T(8,128)(2,1)S(1)} %get-tuple-element.278), channel_id=1, source_target_pairs={{0,15},{1,0},{2,1},{3,2},{4,3},{5,4},{6,5},{7,6},{8,7},{9,8},{10,9... | collective-permute-start | bytes 3145736 | tf_op jit(solution)/shard_map/ppermute | solution.py:14
  320.0 6.9 %copy-start.5 = (bf16[2,128,1024]{1,2,0:T(8,128)(2,1)S(1)}, bf16[2,128,1024]{1,2,0:T(8,128)(2,1)}, u32[]{:S(2)}) copy-start(bf16[2,128,1024]{1,2,0:T(8,128)(2,1)} %get-tuple-element.126) | copy-start | bytes 1572868
  320.0 7.9 %copy-start.10 = (bf16[2,128,1024]{1,2,0:T(8,128)(2,1)S(1)}, bf16[2,128,1024]{1,2,0:T(8,128)(2,1)}, u32[]{:S(2)}) copy-start(bf16[2,128,1024]{1,2,0:T(8,128)(2,1)} %get-tuple-element.129) | copy-start | bytes 1572868
  324.4 25.0 %collective-permute-start.5 = (bf16[2,256,1024]{2,1,0:T(8,128)(2,1)}, bf16[2,256,1024]{2,1,0:T(8,128)(2,1)S(1)}, u32[]{:S(2)}, u32[]{:S(2)}) collective-permute-start(bf16[2,256,1024]{2,1,0:T(8,128)(2,1)} %get-tuple-element.275), channel_id=1, source_target_pairs={{0,1},{1,2},{2,3},{3,4},{4,5},{5,6},{6,7},{7,8},{8,9},{9,10},{10,1... | collective-permute-start | bytes 3145736 | tf_op jit(solution)/shard_map/ppermute | solution.py:14
  326.9 22.5 %collective-permute-start.7 = (bf16[2,256,1024]{2,1,0:T(8,128)(2,1)}, bf16[2,256,1024]{2,1,0:T(8,128)(2,1)S(1)}, u32[]{:S(2)}, u32[]{:S(2)}) collective-permute-start(bf16[2,256,1024]{2,1,0:T(8,128)(2,1)} %get-tuple-element.276), channel_id=1, source_target_pairs={{0,15},{1,0},{2,1},{3,2},{4,3},{5,4},{6,5},{7,6},{8,7},{9,8},{10,9... | collective-permute-start | bytes 3145736 | tf_op jit(solution)/shard_map/ppermute | solution.py:14
  (3 other events, 3.6 us)
where the time goes:
time: 355 us; the launch traced here: 353 us
  local copies, waits for them, and re-layouts  161 us (45%)
  waiting for transfers between devices  85.1 us (24%)
  other arithmetic  58.6 us (17%)
  matrix products  26.4 us (7%)
  loops' own time  11.1 us (3%)
  starting transfers between devices  9.76 us (3%)
    ppermute x8, waiting for transfers between devices, shifted(): lax.ppermute(x, axis, [(i, (i + by) % length) for i in range(length)])  85.1 us
    squeeze x8, local copies, waits for them, and re-layouts, split_heads(): return matrix.reshape(matrix.shape[0], HEADS, matrix.shape[1] // HEADS)  24.3 us
    slice x6, local copies, waits for them, and re-layouts, block_inputs(): k_all = split_heads(picked[0].reshape(list_width * blk_len, model_width))  23.7 us
    slice x6, local copies, waits for them, and re-layouts, block_inputs(): v_all = split_heads(picked[1].reshape(list_width * blk_len, model_width))  23.6 us
    gather x4, local copies, waits for them, and re-layouts, block_inputs(): picked = window_tiles[:, slots]  21 us
    scatter-add x2, other arithmetic, outer_step(): grad_win.at[1, slots].add(dv_all.reshape(list_width, blk_len, model_width))  19 us
    scatter-add x2, other arithmetic, outer_step(): grad_win.at[0, slots].add(dk_all.reshape(list_width, blk_len, model_width))  18.8 us
    while x28, local copies, waits for them, and re-layouts  18.3 us
  transfers between devices with their start and end apart: 8, of which 6 were waited for; matrix products, arithmetic and copies ran while one was open for 2% of the time, Pallas kernels for 0%

commit v1 on v0

v1 whole, which is shorter than its diff:
```python
import functools
import math

import jax
import jax.numpy as jnp
from jax import lax
from jax.experimental import pallas as pl
from jax.experimental.pallas import tpu as pltpu
from jax.sharding import PartitionSpec as P

HEADS = 16
LANES = 128
AHEAD = 4
SLOTS = 5
MASKED = -1e30
F32 = jnp.float32
BF16 = jnp.bfloat16


def matmul(a, b):
    return jnp.dot(a, b, preferred_element_type=F32)


def matmul_nt(a, b):
    return lax.dot_general(a, b, (((1,), (1,)), ((), ())), preferred_element_type=F32)


def kernel(
    shards, own_blocks, list_width, head_dim,
    nbr_ref, cnt_ref, q_ref, k_ref, v_ref, g_ref,
    out_ref, dq_ref, dk_ref, dv_ref,
    kv, acc, sib_s, sib_r, far_s, far_r, near_s, near_r,
    bias, s_scr, e_scr, d_scr, sends, recvs,
):
    rows, width = q_ref.shape
    chunks = width // LANES
    pack = LANES // head_dim
    blk_len = rows // own_blocks
    factor = 1.0 / math.sqrt(head_dim)
    chips = shards // 2

    me = lax.axis_index("blk")
    core = lax.rem(me, 2)
    chip = lax.div(me, 2)
    odd = lax.rem(chip, 2)
    step = 1 - 2 * odd
    near_chip = chip + step
    far_chip = lax.rem(chip - step + chips, chips)
    ahead_chip = lax.rem(chip + 2 * step + chips, chips)
    back_chip = lax.rem(chip - 2 * step + chips, chips)
    sibling = 2 * chip + 1 - core
    near = 2 * near_chip + core
    ahead = 2 * ahead_chip + core
    back = 2 * back_chip + core
    mix = lax.rem(core + chip, 2)
    lent = 2 + mix

    barrier = pltpu.get_barrier_semaphore()
    for other in (sibling, near, ahead, back):
        pl.semaphore_signal(
            barrier, inc=1, device_id={"blk": other}, device_id_type=pl.DeviceIdType.MESH
        )

    for c in range(chunks):
        kv[0, c, 0] = k_ref[:, c * LANES:(c + 1) * LANES]
        kv[0, c, 1] = v_ref[:, c * LANES:(c + 1) * LANES]

    row_id = lax.broadcasted_iota(jnp.int32, bias.shape, 0)
    lane_blk = lax.broadcasted_iota(jnp.int32, bias.shape, 1) // blk_len
    borrowed_chip = near_chip * mix + far_chip * (1 - mix)
    borrowed = 2 * borrowed_chip + 1 - core
    key_blk = jnp.full(bias.shape, -2, jnp.int32)
    for slot, dev in enumerate((me, sibling, near, 2 * far_chip + core, borrowed)):
        for b in range(own_blocks):
            key_blk = jnp.where(row_id == slot * own_blocks + b, dev * own_blocks + b, key_blk)
    allowed = jnp.zeros(bias.shape, jnp.int32)
    for s in range(list_width):
        entry = jnp.full(bias.shape, -1, jnp.int32)
        for b in range(own_blocks):
            live = jnp.where(s < cnt_ref[b], nbr_ref[b, s], -1)
            entry = jnp.where(lane_blk == b, live, entry)
        allowed = jnp.where(entry == key_blk, 1, allowed)
    bias[...] = jnp.where(allowed == 1, 0.0, MASKED).astype(F32)

    pl.semaphore_wait(barrier, 4)

    def remote(stream, src, dst, c, dev):
        return pltpu.make_async_remote_copy(
            src_ref=src,
            dst_ref=dst,
            send_sem=sends.at[stream, c],
            recv_sem=recvs.at[stream, c],
            device_id={"blk": dev},
            device_id_type=pl.DeviceIdType.MESH,
        )

    def to_near(c):
        return remote(0, kv.at[0, c], kv.at[2, c], c, near)

    def to_sibling(c):
        return remote(1, kv.at[0, c], kv.at[1, c], c, sibling)

    def relay(c):
        return remote(2, kv.at[2, c], kv.at[3, c], c, ahead)

    def lend(c):
        return remote(3, kv.at[lent, c], kv.at[4, c], c, sibling)

    def grad_sibling(c):
        return remote(4, sib_s.at[c], sib_r.at[c], c, sibling)

    def grad_far(c):
        return remote(5, far_s.at[c], far_r.at[c], c, back)

    def grad_near(c):
        return remote(6, near_s.at[c], near_r.at[c], c, near)

    def compute(c):
        cols = pl.ds(pl.multiple_of(c * LANES, LANES), LANES)
        q_t = q_ref[:, cols].T
        g_t = g_ref[:, cols].T
        out_parts, dq_parts, qs_parts, gs_parts = [], [], [], []
        for h in range(pack):
            lo, hi = h * head_dim, (h + 1) * head_dim

            def padded(x):
                pieces = []
                if lo:
                    pieces.append(jnp.zeros((lo, rows), x.dtype))
                pieces.append(x)
                if hi < LANES:
                    pieces.append(jnp.zeros((LANES - hi, rows), x.dtype))
                return jnp.concatenate(pieces, axis=0)

            q_h = q_t[lo:hi]
            g_h = g_t[lo:hi]
            q_pad = padded(q_h)
            g_pad = padded(g_h)
            here = slice(h * rows, (h + 1) * rows)
            top = None
            for slot in range(SLOTS):
                scores = matmul(kv[slot, c, 0], q_pad)
                for b in range(own_blocks):
                    r = slot * own_blocks + b
                    part = scores[b * blk_len:(b + 1) * blk_len] + bias[r:r + 1, :]
                    s_scr[r * blk_len:(r + 1) * blk_len, :] = part
                    part_top = jnp.max(part, axis=0, keepdims=True)
                    top = part_top if top is None else jnp.maximum(top, part_top)
            total = jnp.zeros((1, rows), F32)
            mixed = jnp.zeros((head_dim, rows), F32)
            for slot in range(SLOTS):
                at = slice(slot * rows, (slot + 1) * rows)
                e = jnp.exp2((s_scr[at, :] - top) * (factor * math.log2(math.e)))
                total = total + jnp.sum(e, axis=0, keepdims=True)
                e_b = e.astype(BF16)
                e_scr[at, here] = e_b
                mixed = mixed + matmul(kv[slot, c, 1].T[lo:hi], e_b)
            inv = 1.0 / total
            out_h = (mixed * inv).astype(BF16)
            g_f = g_h.astype(F32)
            delta = jnp.sum(g_f * out_h.astype(F32), axis=0, keepdims=True)
            dq = jnp.zeros((head_dim, rows), F32)
            for slot in range(SLOTS):
                at = slice(slot * rows, (slot + 1) * rows)
                dprobs = matmul(kv[slot, c, 1], g_pad)
                d_b = (e_scr[at, here].astype(F32) * (dprobs - delta)).astype(BF16)
                d_scr[at, here] = d_b
                dq = dq + matmul(kv[slot, c, 0].T[lo:hi], d_b)
            out_parts.append(out_h)
            dq_parts.append((dq * (inv * factor)).astype(BF16))
            gs_parts.append(padded((g_f * inv).astype(BF16)))
            qs_parts.append(padded((q_h.astype(F32) * (inv * factor)).astype(BF16)))
        out_ref[:, cols] = jnp.concatenate(out_parts, axis=0).T
        dq_ref[:, cols] = jnp.concatenate(dq_parts, axis=0).T
        q_all = jnp.concatenate(qs_parts, axis=1)
        g_all = jnp.concatenate(gs_parts, axis=1)
        for slot in range(SLOTS):
            at = slice(slot * rows, (slot + 1) * rows)
            dk = matmul_nt(d_scr[at, :], q_all)
            dv = matmul_nt(e_scr[at, :], g_all)
            if slot in (1, 4):
                sib_s[c, slot // 4, 0] = dk.astype(BF16)
                sib_s[c, slot // 4, 1] = dv.astype(BF16)
            else:
                acc[c, max(slot - 1, 0), 0] = dk
                acc[c, max(slot - 1, 0), 1] = dv

    for c in range(AHEAD):
        to_near(c).start()
        to_sibling(c).start()

    def body(t, carry):
        @pl.when(t + AHEAD < chunks)
        def _():
            to_near(t + AHEAD).start()
            to_sibling(t + AHEAD).start()

        @pl.when(t < chunks)
        def _():
            to_near(t).wait_recv()
            relay(t).start()

        @pl.when((t >= 1) & (t < chunks + 1))
        def _():
            relay(t - 1).wait_recv()
            lend(t - 1).start()

        @pl.when((t >= 3) & (t < chunks + 3))
        def _():
            c = t - 3
            grad_sibling(c).wait_recv()
            acc[c, lent - 1] += sib_r[c, 1].astype(F32)
            far_s[c] = acc[c, 2].astype(BF16)
            grad_far(c).start()

        @pl.when((t >= 4) & (t < chunks + 4))
        def _():
            c = t - 4
            grad_far(c).wait_recv()
            near_s[c] = (acc[c, 1] + far_r[c].astype(F32)).astype(BF16)
            grad_near(c).start()

        @pl.when(t >= 5)
        def _():
            c = t - 5
            cols = pl.ds(pl.multiple_of(c * LANES, LANES), LANES)
            grad_near(c).wait_recv()
            final = acc[c, 0] + sib_r[c, 0].astype(F32) + near_r[c].astype(F32)
            dk_ref[:, cols] = final[0].astype(BF16)
            dv_ref[:, cols] = final[1].astype(BF16)

        @pl.when((t >= 2) & (t < chunks + 2))
        def _():
            c = t - 2
            to_sibling(c).wait_recv()
            lend(c).wait_recv()
            compute(c)
            grad_sibling(c).start()

        return carry

    lax.fori_loop(0, chunks + 5, body, 0)

    def finish(c, carry):
        for copy in (to_near, to_sibling, relay, lend, grad_sibling, grad_far, grad_near):
            copy(c).wait_send()
        return carry

    lax.fori_loop(0, chunks, finish, 0)


def local(shards, query, key_in, value, grad_out, neighbors, counts):
    rows, width = query.shape
    own_blocks, list_width = neighbors.shape
    head_dim = width // HEADS
    chunks = width // LANES
    pack = LANES // head_dim
    tile = (2, rows, LANES)
    vmem = pl.BlockSpec(memory_space=pltpu.VMEM)
    smem = pl.BlockSpec(memory_space=pltpu.SMEM)
    shape = jax.ShapeDtypeStruct((rows, width), query.dtype)
    bias_rows = -(-SLOTS * own_blocks // 8) * 8
    return pl.pallas_call(
        functools.partial(kernel, shards, own_blocks, list_width, head_dim),
        out_shape=(shape,) * 4,
        in_specs=[smem, smem, vmem, vmem, vmem, vmem],
        out_specs=(vmem,) * 4,
        scratch_shapes=[
            pltpu.VMEM((SLOTS, chunks) + tile, BF16),
            pltpu.VMEM((chunks, 3) + tile, F32),
            pltpu.VMEM((chunks, 2) + tile, BF16),
            pltpu.VMEM((chunks, 2) + tile, BF16),
            pltpu.VMEM((chunks,) + tile, BF16),
            pltpu.VMEM((chunks,) + tile, BF16),
            pltpu.VMEM((chunks,) + tile, BF16),
            pltpu.VMEM((chunks,) + tile, BF16),
            pltpu.VMEM((bias_rows, rows), F32),
            pltpu.VMEM((SLOTS * rows, rows), F32),
            pltpu.VMEM((SLOTS * rows, pack * rows), BF16),
            pltpu.VMEM((SLOTS * rows, pack * rows), BF16),
            pltpu.SemaphoreType.DMA((7, chunks)),
            pltpu.SemaphoreType.DMA((7, chunks)),
        ],
        compiler_params=pltpu.CompilerParams(
            collective_id=0, has_side_effects=True, vmem_limit_bytes=52 * 1024 * 1024
        ),
        name="graph_attention",
    )(neighbors, counts, query, key_in, value, grad_out)


def solution(mesh):
    rows = P(("groups", "blk"), None)
    return jax.shard_map(
        functools.partial(local, mesh.shape["blk"]),
        mesh=mesh,
        in_specs=(rows, rows, rows, rows, rows, P(("groups", "blk"))),
        out_specs=(rows,) * 4,
        check_vma=False,
    )
```

time: 355 us -> 81.5 us (0.23)
  local copies, waits for them, and re-layouts: 161 us -> 4.94 us
  waiting for transfers between devices: 85.1 us -> 0 us
  Pallas kernels: 0 us -> 74.3 us
  other arithmetic: 58.6 us -> 0 us
  matrix products: 26.4 us -> 0 us
  loops' own time: 11.1 us -> 0 us
  starting transfers between devices: 9.76 us -> 0 us
    ppermute x8 -> x0, waiting for transfers between devices: 85.1 us -> none  [shifted(): lax.ppermute(x, axis, [(i, (i + by) % length) for i in range(length)])]
    pallas_call x0 -> x1, Pallas kernels: none -> 74.3 us  [local(): pl.pallas_call(functools.partial(kernel, shards, own_blocks, list_width,...]
    slice x13 -> x0, local copies, waits for them, and re-layouts: 47.5 us -> none  [the longest x6 23.7 us: block_inputs(): k_all = split_heads(picked[0].reshape(list_width * blk_len, model_width))]
    scatter-add x4 -> x0, other arithmetic: 37.8 us -> none  [the longest x2 19 us: outer_step(): grad_win.at[1, slots].add(dv_all.reshape(list_width, blk_len, model_width))]
    dot_general x14 -> x0, matrix products: 26.4 us -> none  [the longest x4 7.94 us: block_inputs(): jnp.einsum('qhd,khd->hqk', q_tile, k_all, preferred_element_type=jnp.floa...]
    squeeze x8 -> x0, local copies, waits for them, and re-layouts: 24.3 us -> none  [split_heads(): return matrix.reshape(matrix.shape[0], HEADS, matrix.shape[1] // HEADS)]
    reshape x4 -> x0, local copies, waits for them, and re-layouts: 21.8 us -> none  [the longest x2 10.9 us: outer_step(): dv_all.reshape(list_width, blk_len, model_width)]
    gather x4 -> x0, local copies, waits for them, and re-layouts: 21 us -> none  [block_inputs(): picked = window_tiles[:, slots]]
  transfers between devices with their start and end apart: 8 -> 0, of which waited for: 6 -> 0; matrix products, arithmetic and copies ran while one was open for 2% -> 0% of each run, Pallas kernels for 0% -> 0%
where the time goes in v1:
time: 81.5 us; the launch traced here: 79.9 us
  Pallas kernels  74.3 us (91%)
  local copies, waits for them, and re-layouts  4.94 us (6%)
    pallas_call x1, Pallas kernels, local(): pl.pallas_call(functools.partial(kernel, shards, own_blocks, list_width,...  74.3 us
    unnamed x10, local copies, waits for them, and re-layouts  4.94 us

profile of v1, /device:TPU:1, one launch (start us, length us, event | category | flops | bytes accessed | tf_op | source)
XLA Modules:
  0.0 79.9 jit_solution(4139538987044289657)
XLA Ops:
  0.6 0.0 copy-start
  0.6 0.7 copy-done
  1.3 0.0 copy-start.1
  1.3 0.7 copy-done.1
  2.0 74.3 %graph_attention.1 = (bf16[256,1024]{1,0:T(8,128)(2,1)S(1)}, bf16[256,1024]{1,0:T(8,128)(2,1)S(1)}, bf16[256,1024]{1,0:T(8,128)(2,1)S(1)}, bf16[256,1024]{1,0:T(8,128)(2,1)}) custom-call(s32[2,8]{1,0:T(2,128)S(1)} %copy-done, s32[2]{0:T(128)S(1)} %copy-done.1, bf16[256,1024]{1,0:T(8,128)(2,1)} %q_ref.1, bf16[256,1024]{1,0:T(8,128)(2,1)} %k_ref.1, ...), custom_call_target="tpu_custom_call" | custom-call | tf_op jit(solution)/shard_map/graph_attention/pallas_call | solution.py:263
  76.2 0.8 copy.14
  77.0 0.8 copy.15
  77.8 0.0 copy-start.2
  77.8 0.8 copy.16
  78.6 0.4 copy-done.2
  79.1 0.8 copy.17
Async XLA Ops:
  0.6 0.7 copy-start
  1.3 0.7 copy-start.1
  77.8 1.2 %copy-start.2 = (bf16[256,1024]{1,0:T(8,128)(2,1)S(1)}, bf16[256,1024]{1,0:T(8,128)(2,1)}, u32[]{:S(2)}) copy-start(bf16[256,1024]{1,0:T(8,128)(2,1)} %get-tuple-element.11) | copy-start | bytes 1572868

commit v2 on v1

--- a/solution.py
+++ b/solution.py
@@ -30,7 +30,7 @@
     nbr_ref, cnt_ref, q_ref, k_ref, v_ref, g_ref,
     out_ref, dq_ref, dk_ref, dv_ref,
     kv, acc, sib_s, sib_r, far_s, far_r, near_s, near_r,
-    bias, s_scr, e_scr, d_scr, sends, recvs,
+    bias, s_scr, e_scr, d_scr, kt_scr, vt_scr, q_scr, g_scr, sends, recvs, loads,
 ):
     rows, width = q_ref.shape
     chunks = width // LANES
@@ -61,9 +61,20 @@
             barrier, inc=1, device_id={"blk": other}, device_id_type=pl.DeviceIdType.MESH
         )
 
+    def load(which, c):
+        cols = pl.ds(pl.multiple_of(c * LANES, LANES), LANES)
+        source = (k_ref, v_ref)[which]
+        return pltpu.make_async_copy(
+            source.at[:, cols], kv.at[0, c, which], loads.at[which, c]
+        )
+
+    load_q = pltpu.make_async_copy(q_ref, q_scr, loads.at[2, 0])
+    load_g = pltpu.make_async_copy(g_ref, g_scr, loads.at[2, 1])
     for c in range(chunks):
-        kv[0, c, 0] = k_ref[:, c * LANES:(c + 1) * LANES]
-        kv[0, c, 1] = v_ref[:, c * LANES:(c + 1) * LANES]
+        load(0, c).start()
+        load(1, c).start()
+    load_q.start()
+    load_g.start()
 
     row_id = lax.broadcasted_iota(jnp.int32, bias.shape, 0)
     lane_blk = lax.broadcasted_iota(jnp.int32, bias.shape, 1) // blk_len
@@ -117,83 +128,82 @@
 
     def compute(c):
         cols = pl.ds(pl.multiple_of(c * LANES, LANES), LANES)
-        q_t = q_ref[:, cols].T
-        g_t = g_ref[:, cols].T
+        q_t = q_scr[:, cols].T
+        g_t = g_scr[:, cols].T
+        keys = kv[:, c, 0].reshape(SLOTS * rows, LANES)
+        vals = kv[:, c, 1].reshape(SLOTS * rows, LANES)
+        for slot in range(SLOTS):
+            at = slice(slot * rows, (slot + 1) * rows)
+            kt_scr[:, at] = kv[slot, c, 0].T
+            vt_scr[:, at] = kv[slot, c, 1].T
+
+        def padded(x, h):
+            pieces = []
+            if h:
+                pieces.append(jnp.zeros((h * head_dim, rows), x.dtype))
+            pieces.append(x)
+            if h < pack - 1:
+                pieces.append(jnp.zeros(((pack - 1 - h) * head_dim, rows), x.dtype))
+            return jnp.concatenate(pieces, axis=0)
+
+        heads = [slice(h * head_dim, (h + 1) * head_dim) for h in range(pack)]
         out_parts, dq_parts, qs_parts, gs_parts = [], [], [], []
         for h in range(pack):
-            lo, hi = h * head_dim, (h + 1) * head_dim
-
-            def padded(x):
-                pieces = []
-                if lo:
-                    pieces.append(jnp.zeros((lo, rows), x.dtype))
-                pieces.append(x)
-                if hi < LANES:
-                    pieces.append(jnp.zeros((LANES - hi, rows), x.dtype))
-                return jnp.concatenate(pieces, axis=0)
-
-            q_h = q_t[lo:hi]
-            g_h = g_t[lo:hi]
-            q_pad = padded(q_h)
-            g_pad = padded(g_h)
+            s_scr[h] = matmul(keys, padded(q_t[heads[h]], h))
+        for h in range(pack):
             here = slice(h * rows, (h + 1) * rows)
             top = None
-            for slot in range(SLOTS):
-                scores = matmul(kv[slot, c, 0], q_pad)
-                for b in range(own_blocks):
-                    r = slot * own_blocks + b
-                    part = scores[b * blk_len:(b + 1) * blk_len] + bias[r:r + 1, :]
-                    s_scr[r * blk_len:(r + 1) * blk_len, :] = part
-                    part_top = jnp.max(part, axis=0, keepdims=True)
-                    top = part_top if top is None else jnp.maximum(top, part_top)
+            for r in range(SLOTS * own_blocks):
+                part = jnp.max(s_scr[h, r * blk_len:(r + 1) * blk_len, :], axis=0, keepdims=True)
+                part = part + bias[r:r + 1, :]
+                top = part if top is None else jnp.maximum(top, part)
             total = jnp.zeros((1, rows), F32)
-            mixed = jnp.zeros((head_dim, rows), F32)
-            for slot in range(SLOTS):
-                at = slice(slot * rows, (slot + 1) * rows)
-                e = jnp.exp2((s_scr[at, :] - top) * (factor * math.log2(math.e)))
+            for r in range(SLOTS * own_blocks):
+                at = slice(r * blk_len, (r + 1) * blk_len)
+                shift = top - bias[r:r + 1, :]
+                e = jnp.exp2((s_scr[h, at, :] - shift) * (factor * math.log2(math.e)))
                 total = total + jnp.sum(e, axis=0, keepdims=True)
-                e_b = e.astype(BF16)
-                e_scr[at, here] = e_b
-                mixed = mixed + matmul(kv[slot, c, 1].T[lo:hi], e_b)
+                e_scr[at, here] = e.astype(BF16)
+            mixed = matmul(vt_scr[heads[h], :], e_scr[:, here])
             inv = 1.0 / total
             out_h = (mixed * inv).astype(BF16)
-            g_f = g_h.astype(F32)
+            g_f = g_t[heads[h]].astype(F32)
             delta = jnp.sum(g_f * out_h.astype(F32), axis=0, keepdims=True)
-            dq = jnp.zeros((head_dim, rows), F32)
-            for slot in range(SLOTS):
-                at = slice(slot * rows, (slot + 1) * rows)
-                dprobs = matmul(kv[slot, c, 1], g_pad)
-                d_b = (e_scr[at, here].astype(F32) * (dprobs - delta)).astype(BF16)
-                d_scr[at, here] = d_b
-                dq = dq + matmul(kv[slot, c, 0].T[lo:hi], d_b)
+            dprobs = matmul(vals, padded(g_t[heads[h]], h))
+            d_scr[:, here] = (e_scr[:, here].astype(F32) * (dprobs - delta)).astype(BF16)
+            dq = matmul(kt_scr[heads[h], :], d_scr[:, here])
             out_parts.append(out_h)
             dq_parts.append((dq * (inv * factor)).astype(BF16))
-            gs_parts.append(padded((g_f * inv).astype(BF16)))
-            qs_parts.append(padded((q_h.astype(F32) * (inv * factor)).astype(BF16)))
+            gs_parts.append(padded((g_f * inv).astype(BF16), h))
+            qs_parts.append(padded((q_t[heads[h]].astype(F32) * (inv * factor)).astype(BF16), h))
         out_ref[:, cols] = jnp.concatenate(out_parts, axis=0).T
         dq_ref[:, cols] = jnp.concatenate(dq_parts, axis=0).T
-        q_all = jnp.concatenate(qs_parts, axis=1)
-        g_all = jnp.concatenate(gs_parts, axis=1)
+        dk = matmul_nt(d_scr[...], jnp.concatenate(qs_parts, axis=1))
+        dv = matmul_nt(e_scr[...], jnp.concatenate(gs_parts, axis=1))
         for slot in range(SLOTS):
             at = slice(slot * rows, (slot + 1) * rows)
-            dk = matmul_nt(d_scr[at, :], q_all)
-            dv = matmul_nt(e_scr[at, :], g_all)
             if slot in (1, 4):
-                sib_s[c, slot // 4, 0] = dk.astype(BF16)
-                sib_s[c, slot // 4, 1] = dv.astype(BF16)
+                sib_s[c, slot // 4, 0] = dk[at].astype(BF16)
+                sib_s[c, slot // 4, 1] = dv[at].astype(BF16)
             else:
-                acc[c, max(slot - 1, 0), 0] = dk
-                acc[c, max(slot - 1, 0), 1] = dv
-
-    for c in range(AHEAD):
+                acc[c, max(slot - 1, 0), 0] = dk[at]
+                acc[c, max(slot - 1, 0), 1] = dv[at]
+
+    def publish(c):
+        load(0, c).wait()
+        load(1, c).wait()
         to_near(c).start()
         to_sibling(c).start()
 
+    for c in range(AHEAD):
+        publish(c)
+    load_q.wait()
+    load_g.wait()
+
     def body(t, carry):
         @pl.when(t + AHEAD < chunks)
         def _():
-            to_near(t + AHEAD).start()
-            to_sibling(t + AHEAD).start()
+            publish(t + AHEAD)
 
         @pl.when(t < chunks)
         def _():
@@ -247,6 +257,15 @@
         return carry
 
     lax.fori_loop(0, chunks, finish, 0)
+
+
+def hand_over(*refs):
+    sems = refs[-1]
+    copies = [pltpu.make_async_copy(refs[i], refs[4 + i], sems.at[i]) for i in range(4)]
+    for copy in copies:
+        copy.start()
+    for copy in copies:
+        copy.wait()
 
 
 def local(shards, query, key_in, value, grad_out, neighbors, counts):
@@ -257,13 +276,14 @@
     pack = LANES // head_dim
     tile = (2, rows, LANES)
     vmem = pl.BlockSpec(memory_space=pltpu.VMEM)
+    hbm = pl.BlockSpec(memory_space=pl.ANY)
     smem = pl.BlockSpec(memory_space=pltpu.SMEM)
     shape = jax.ShapeDtypeStruct((rows, width), query.dtype)
     bias_rows = -(-SLOTS * own_blocks // 8) * 8
-    return pl.pallas_call(
+    results = pl.pallas_call(
         functools.partial(kernel, shards, own_blocks, list_width, head_dim),
         out_shape=(shape,) * 4,
-        in_specs=[smem, smem, vmem, vmem, vmem, vmem],
+        in_specs=[smem, smem, hbm, hbm, hbm, hbm],
         out_specs=(vmem,) * 4,
         scratch_shapes=[
             pltpu.VMEM((SLOTS, chunks) + tile, BF16),
@@ -275,17 +295,31 @@
             pltpu.VMEM((chunks,) + tile, BF16),
             pltpu.VMEM((chunks,) + tile, BF16),
             pltpu.VMEM((bias_rows, rows), F32),
-            pltpu.VMEM((SLOTS * rows, rows), F32),
+            pltpu.VMEM((pack, SLOTS * rows, rows), F32),
             pltpu.VMEM((SLOTS * rows, pack * rows), BF16),
             pltpu.VMEM((SLOTS * rows, pack * rows), BF16),
+            pltpu.VMEM((LANES, SLOTS * rows), BF16),
+            pltpu.VMEM((LANES, SLOTS * rows), BF16),
+            pltpu.VMEM((rows, width), BF16),
+            pltpu.VMEM((rows, width), BF16),
             pltpu.SemaphoreType.DMA((7, chunks)),
             pltpu.SemaphoreType.DMA((7, chunks)),
+            pltpu.SemaphoreType.DMA((3, chunks)),
         ],
         compiler_params=pltpu.CompilerParams(
-            collective_id=0, has_side_effects=True, vmem_limit_bytes=52 * 1024 * 1024
+            collective_id=0, has_side_effects=True, vmem_limit_bytes=56 * 1024 * 1024
         ),
         name="graph_attention",
     )(neighbors, counts, query, key_in, value, grad_out)
+    return pl.pallas_call(
+        hand_over,
+        out_shape=(shape,) * 4,
+        in_specs=[hbm] * 4,
+        out_specs=(hbm,) * 4,
+        scratch_shapes=[pltpu.SemaphoreType.DMA((4,))],
+        compiler_params=pltpu.CompilerParams(vmem_limit_bytes=60 * 1024 * 1024),
+        name="hand_over",
+    )(*results)
 
 
 def solution(mesh):

time: 81.5 us -> 140 us (1.72)
  Pallas kernels: 74.3 us -> 138 us
  local copies, waits for them, and re-layouts: 4.94 us -> 0 us
    pallas_call x0 -> x1, Pallas kernels: none -> 64.7 us  [local(): pl.pallas_call(hand_over, out_shape=(shape,) * 4, in_specs=[hbm] * 4, out...]
    unnamed x10 -> x0, local copies, waits for them, and re-layouts: 4.94 us -> none
where the time goes in v2:
time: 140 us; the launch traced here: 138 us
  Pallas kernels  138 us (99%)
    pallas_call x1, Pallas kernels, local(): pl.pallas_call(functools.partial(kernel, shards, own_blocks, list_width,...  73.1 us
    pallas_call x1, Pallas kernels, local(): pl.pallas_call(hand_over, out_shape=(shape,) * 4, in_specs=[hbm] * 4, out...  64.7 us

profile of v2, /device:TPU:1, one launch (start us, length us, event | category | flops | bytes accessed | tf_op | source)
XLA Modules:
  0.0 138.4 jit_solution(9465400910707674238)
XLA Ops:
  0.6 73.1 %graph_attention.1 = (bf16[256,1024]{1,0:T(8,128)(2,1)}, bf16[256,1024]{1,0:T(8,128)(2,1)}, bf16[256,1024]{1,0:T(8,128)(2,1)}, bf16[256,1024]{1,0:T(8,128)(2,1)}) custom-call(s32[2,8]{1,0:T(2,128)} %nbr_ref.1, s32[2]{0:T(128)} %cnt_ref.1, bf16[256,1024]{1,0:T(8,128)(2,1)} %q_ref.1, bf16[256,1024]{1,0:T(8,128)(2,1)} %k_ref.1, bf16[256,1024]{1,0:T(8,128)(2,1)} %v_ref.1, ...), custom_call_target="tpu_custom_call" | custom-call | tf_op jit(solution)/shard_map/graph_attention/pallas_call | solution.py:283
  73.8 64.7 %hand_over.1 = (bf16[256,1024]{1,0:T(8,128)(2,1)}, bf16[256,1024]{1,0:T(8,128)(2,1)}, bf16[256,1024]{1,0:T(8,128)(2,1)}, bf16[256,1024]{1,0:T(8,128)(2,1)}) custom-call(bf16[256,1024]{1,0:T(8,128)(2,1)} %get-tuple-element.8.refs_0_, bf16[256,1024]{1,0:T(8,128)(2,1)} %get-tuple-element.9.refs_1_, bf16[256,1024]{1,0:T(8,128)(2,1)} %get-tuple-element.10.refs_2_, ...), custom_call_target="tpu_custom_call" | custom-call | tf_op jit(solution)/shard_map/hand_over/pallas_call | solution.py:314

commit v3 on v2

v3 whole, which is shorter than its diff:
```python
import functools
import math

import jax
import jax.numpy as jnp
from jax import lax
from jax.experimental import pallas as pl
from jax.experimental.pallas import tpu as pltpu
from jax.sharding import PartitionSpec as P

HEADS = 16
LANES = 128
AHEAD = 3
SLOTS = 5
MASKED = -1e30
F32 = jnp.float32
BF16 = jnp.bfloat16


def matmul(a, b):
    return jnp.dot(a, b, preferred_element_type=F32)


def matmul_nt(a, b):
    return lax.dot_general(a, b, (((1,), (1,)), ((), ())), preferred_element_type=F32)


def kernel(
    shards, own_blocks, list_width, head_dim,
    nbr_ref, cnt_ref, q_ref, k_ref, v_ref, g_ref,
    out_ref, dq_ref, dk_ref, dv_ref,
    kv, acc, sib_s, sib_r, far_s, far_r, near_s, near_r,
    bias, s_scr, e_scr, d_scr, kt_scr, vt_scr, q_scr, g_scr,
    q_t, g_t, out_t, dq_t, qs_scr, gs_scr, sends, recvs, loads,
):
    rows, width = q_ref.shape
    chunks = width // LANES
    pack = LANES // head_dim
    blk_len = rows // own_blocks
    factor = 1.0 / math.sqrt(head_dim)
    chips = shards // 2

    me = lax.axis_index("blk")
    core = lax.rem(me, 2)
    chip = lax.div(me, 2)
    odd = lax.rem(chip, 2)
    step = 1 - 2 * odd
    near_chip = chip + step
    far_chip = lax.rem(chip - step + chips, chips)
    ahead_chip = lax.rem(chip + 2 * step + chips, chips)
    back_chip = lax.rem(chip - 2 * step + chips, chips)
    sibling = 2 * chip + 1 - core
    near = 2 * near_chip + core
    ahead = 2 * ahead_chip + core
    back = 2 * back_chip + core
    mix = lax.rem(core + chip, 2)
    lent = 2 + mix

    barrier = pltpu.get_barrier_semaphore()
    for other in (sibling, near, ahead, back):
        pl.semaphore_signal(
            barrier, inc=1, device_id={"blk": other}, device_id_type=pl.DeviceIdType.MESH
        )

    def load(which, c):
        cols = pl.ds(pl.multiple_of(c * LANES, LANES), LANES)
        source = (k_ref, v_ref)[which]
        return pltpu.make_async_copy(
            source.at[:, cols], kv.at[0, c, which], loads.at[which, c]
        )

    load_q = pltpu.make_async_copy(q_ref, q_scr, loads.at[2, 0])
    load_g = pltpu.make_async_copy(g_ref, g_scr, loads.at[2, 1])
    for c in range(chunks):
        load(0, c).start()
        load(1, c).start()
    load_q.start()
    load_g.start()

    row_id = lax.broadcasted_iota(jnp.int32, bias.shape, 0)
    lane_blk = lax.broadcasted_iota(jnp.int32, bias.shape, 1) // blk_len
    borrowed_chip = near_chip * mix + far_chip * (1 - mix)
    borrowed = 2 * borrowed_chip + 1 - core
    key_blk = jnp.full(bias.shape, -2, jnp.int32)
    for slot, dev in enumerate((me, sibling, near, 2 * far_chip + core, borrowed)):
        for b in range(own_blocks):
            key_blk = jnp.where(row_id == slot * own_blocks + b, dev * own_blocks + b, key_blk)
    allowed = jnp.zeros(bias.shape, jnp.int32)
    for s in range(list_width):
        entry = jnp.full(bias.shape, -1, jnp.int32)
        for b in range(own_blocks):
            live = jnp.where(s < cnt_ref[b], nbr_ref[b, s], -1)
            entry = jnp.where(lane_blk == b, live, entry)
        allowed = jnp.where(entry == key_blk, 1, allowed)
    bias[...] = jnp.where(allowed == 1, 0.0, MASKED).astype(F32)

    pl.semaphore_wait(barrier, 4)

    def remote(stream, src, dst, c, part, dev):
        return pltpu.make_async_remote_copy(
            src_ref=src,
            dst_ref=dst,
            send_sem=sends.at[stream, part, c],
            recv_sem=recvs.at[stream, part, c],
            device_id={"blk": dev},
            device_id_type=pl.DeviceIdType.MESH,
        )

    def to_near(c, part):
        return remote(0, kv.at[0, c, part], kv.at[2, c, part], c, part, near)

    def to_sibling(c, part):
        return remote(1, kv.at[0, c, part], kv.at[1, c, part], c, part, sibling)

    def relay(c, part):
        return remote(2, kv.at[2, c, part], kv.at[3, c, part], c, part, ahead)

    def lend(c, part):
        return remote(3, kv.at[lent, c, part], kv.at[4, c, part], c, part, sibling)

    def grad_sibling(c, part):
        return remote(4, sib_s.at[c, part], sib_r.at[c, part], c, part, sibling)

    def grad_far(c, part):
        return remote(5, far_s.at[c, part], far_r.at[c, part], c, part, back)

    def grad_near(c, part):
        return remote(6, near_s.at[c, part], near_r.at[c, part], c, part, near)

    def columns(c):
        return pl.ds(pl.multiple_of(c * LANES, LANES), LANES)

    def publish(c):
        for part in range(2):
            load(part, c).wait()
            to_near(c, part).start()
            to_sibling(c, part).start()

    def pass_on(c):
        for part in range(2):
            to_near(c, part).wait_recv()
            relay(c, part).start()

    def lend_on(c):
        for part in range(2):
            relay(c, part).wait_recv()
            lend(c, part).start()

    def send_far(c):
        for part in range(2):
            grad_sibling(c, part).wait_recv()
            acc[c, lent - 1, part] += sib_r[c, part, 1].astype(F32)
            far_s[c, part] = acc[c, 2, part].astype(BF16)
            grad_far(c, part).start()

    def send_near(c):
        for part in range(2):
            grad_far(c, part).wait_recv()
            near_s[c, part] = (acc[c, 1, part] + far_r[c, part].astype(F32)).astype(BF16)
            grad_near(c, part).start()

    def close(c):
        for part, result in enumerate((dk_ref, dv_ref)):
            grad_near(c, part).wait_recv()
            final = acc[c, 0, part] + sib_r[c, part, 0].astype(F32)
            result[:, columns(c)] = (final + near_r[c, part].astype(F32)).astype(BF16)

    def exchange(c):
        @pl.when(c + AHEAD < chunks)
        def _():
            publish(c + AHEAD)

        @pl.when(c + 2 < chunks)
        def _():
            pass_on(c + 2)

        @pl.when(c + 1 < chunks)
        def _():
            lend_on(c + 1)

        @pl.when(c >= 1)
        def _():
            send_far(c - 1)

        @pl.when(c >= 2)
        def _():
            send_near(c - 2)

        @pl.when(c >= 3)
        def _():
            close(c - 3)

    def padded(x, h):
        pieces = []
        if h:
            pieces.append(jnp.zeros((h * head_dim, rows), x.dtype))
        pieces.append(x)
        if h < pack - 1:
            pieces.append(jnp.zeros(((pack - 1 - h) * head_dim, rows), x.dtype))
        return jnp.concatenate(pieces, axis=0)

    def one_head(c, h):
        head = slice(h * head_dim, (h + 1) * head_dim)
        here = slice(h * rows, (h + 1) * rows)
        keys = kv[:, c, 0].reshape(SLOTS * rows, LANES)
        vals = kv[:, c, 1].reshape(SLOTS * rows, LANES)
        q_h = q_t[head, :]
        g_h = g_t[head, :]
        s_scr[h] = matmul(keys, padded(q_h, h))
        top = None
        for r in range(SLOTS * own_blocks):
            part = jnp.max(s_scr[h, r * blk_len:(r + 1) * blk_len, :], axis=0, keepdims=True)
            part = part + bias[r:r + 1, :]
            top = part if top is None else jnp.maximum(top, part)
        total = jnp.zeros((1, rows), F32)
        for r in range(SLOTS * own_blocks):
            at = slice(r * blk_len, (r + 1) * blk_len)
            shift = top - bias[r:r + 1, :]
            e = jnp.exp2((s_scr[h, at, :] - shift) * (factor * math.log2(math.e)))
            total = total + jnp.sum(e, axis=0, keepdims=True)
            e_scr[at, here] = e.astype(BF16)
        mixed = matmul(vt_scr[head, :], e_scr[:, here])
        inv = 1.0 / total
        out_h = (mixed * inv).astype(BF16)
        g_f = g_h.astype(F32)
        delta = jnp.sum(g_f * out_h.astype(F32), axis=0, keepdims=True)
        dprobs = matmul(vals, padded(g_h, h))
        d_scr[:, here] = (e_scr[:, here].astype(F32) * (dprobs - delta)).astype(BF16)
        dq = matmul(kt_scr[head, :], d_scr[:, here])
        out_t[head, :] = out_h
        dq_t[head, :] = (dq * (inv * factor)).astype(BF16)
        gs_scr[:, here] = padded((g_f * inv).astype(BF16), h)
        qs_scr[:, here] = padded((q_h.astype(F32) * (inv * factor)).astype(BF16), h)

    for c in range(AHEAD):
        publish(c)
    load_q.wait()
    load_g.wait()
    pass_on(0)
    pass_on(1)
    lend_on(0)

    def body(c, carry):
        cols = columns(c)
        q_t[...] = q_scr[:, cols].T
        g_t[...] = g_scr[:, cols].T
        for part in range(2):
            to_sibling(c, part).wait_recv()
            lend(c, part).wait_recv()
        for slot in range(SLOTS):
            at = slice(slot * rows, (slot + 1) * rows)
            kt_scr[:, at] = kv[slot, c, 0].T
            vt_scr[:, at] = kv[slot, c, 1].T
        for h in range(pack):
            if h == pack // 2:
                exchange(c)
            one_head(c, h)
        for part, (left, right) in enumerate(((d_scr, qs_scr), (e_scr, gs_scr))):
            grad = matmul_nt(left[...], right[...])
            for slot in range(SLOTS):
                at = slice(slot * rows, (slot + 1) * rows)
                if slot in (1, 4):
                    sib_s[c, part, slot // 4] = grad[at].astype(BF16)
                else:
                    acc[c, max(slot - 1, 0), part] = grad[at]
            grad_sibling(c, part).start()
        out_ref[:, cols] = out_t[...].T
        dq_ref[:, cols] = dq_t[...].T
        return carry

    lax.fori_loop(0, chunks, body, 0)

    send_far(chunks - 1)
    send_near(chunks - 2)
    close(chunks - 3)
    send_near(chunks - 1)
    close(chunks - 2)
    close(chunks - 1)

    def finish(c, carry):
        for copy in (to_near, to_sibling, relay, lend, grad_sibling, grad_far, grad_near):
            for part in range(2):
                copy(c, part).wait_send()
        return carry

    lax.fori_loop(0, chunks, finish, 0)


def hand_over(*refs):
    sources, results, held, sems = refs[:4], refs[4:8], refs[8], refs[9]
    reads = [pltpu.make_async_copy(sources[i], held.at[i], sems.at[0, i]) for i in range(4)]
    writes = [pltpu.make_async_copy(held.at[i], results[i], sems.at[1, i]) for i in range(4)]
    for read in reads:
        read.start()
    for read, write in zip(reads, writes):
        read.wait()
        write.start()
    for write in writes:
        write.wait()


def local(shards, query, key_in, value, grad_out, neighbors, counts):
    rows, width = query.shape
    own_blocks, list_width = neighbors.shape
    head_dim = width // HEADS
    chunks = width // LANES
    pack = LANES // head_dim
    tile = (2, rows, LANES)
    vmem = pl.BlockSpec(memory_space=pltpu.VMEM)
    hbm = pl.BlockSpec(memory_space=pl.ANY)
    smem = pl.BlockSpec(memory_space=pltpu.SMEM)
    shape = jax.ShapeDtypeStruct((rows, width), query.dtype)
    bias_rows = -(-SLOTS * own_blocks // 8) * 8
    results = pl.pallas_call(
        functools.partial(kernel, shards, own_blocks, list_width, head_dim),
        out_shape=(shape,) * 4,
        in_specs=[smem, smem, hbm, hbm, hbm, hbm],
        out_specs=(vmem,) * 4,
        scratch_shapes=[
            pltpu.VMEM((SLOTS, chunks) + tile, BF16),
            pltpu.VMEM((chunks, 3) + tile, F32),
            pltpu.VMEM((chunks, 2) + tile, BF16),
            pltpu.VMEM((chunks, 2) + tile, BF16),
            pltpu.VMEM((chunks,) + tile, BF16),
            pltpu.VMEM((chunks,) + tile, BF16),
            pltpu.VMEM((chunks,) + tile, BF16),
            pltpu.VMEM((chunks,) + tile, BF16),
            pltpu.VMEM((bias_rows, rows), F32),
            pltpu.VMEM((pack, SLOTS * rows, rows), F32),
            pltpu.VMEM((SLOTS * rows, pack * rows), BF16),
            pltpu.VMEM((SLOTS * rows, pack * rows), BF16),
            pltpu.VMEM((LANES, SLOTS * rows), BF16),
            pltpu.VMEM((LANES, SLOTS * rows), BF16),
            pltpu.VMEM((rows, width), BF16),
            pltpu.VMEM((rows, width), BF16),
            pltpu.VMEM((LANES, rows), BF16),
            pltpu.VMEM((LANES, rows), BF16),
            pltpu.VMEM((LANES, rows), BF16),
            pltpu.VMEM((LANES, rows), BF16),
            pltpu.VMEM((LANES, pack * rows), BF16),
            pltpu.VMEM((LANES, pack * rows), BF16),
            pltpu.SemaphoreType.DMA((7, 2, chunks)),
            pltpu.SemaphoreType.DMA((7, 2, chunks)),
            pltpu.SemaphoreType.DMA((3, chunks)),
        ],
        compiler_params=pltpu.CompilerParams(
            collective_id=0, has_side_effects=True, vmem_limit_bytes=56 * 1024 * 1024
        ),
        name="graph_attention",
    )(neighbors, counts, query, key_in, value, grad_out)
    return pl.pallas_call(
        hand_over,
        out_shape=(shape,) * 4,
        in_specs=[hbm] * 4,
        out_specs=(hbm,) * 4,
        scratch_shapes=[
            pltpu.VMEM((4, rows, width), query.dtype),
            pltpu.SemaphoreType.DMA((2, 4)),
        ],
        compiler_params=pltpu.CompilerParams(vmem_limit_bytes=60 * 1024 * 1024),
        name="hand_over",
    )(*results)


def solution(mesh):
    rows = P(("groups", "blk"), None)
    return jax.shard_map(
        functools.partial(local, mesh.shape["blk"]),
        mesh=mesh,
        in_specs=(rows, rows, rows, rows, rows, P(("groups", "blk"))),
        out_specs=(rows,) * 4,
        check_vma=False,
    )
```

time: 140 us -> 78.3 us (0.56)
  Pallas kernels: 138 us -> 76.7 us
    pallas_call x1, Pallas kernels: 64.7 us -> 2.42 us  [local(): pl.pallas_call(hand_over, out_shape=(shape,) * 4, in_specs=[hbm] * 4, out...]
where the time goes in v3:
time: 78.3 us; the launch traced here: 77.4 us
  Pallas kernels  76.7 us (98%)
    pallas_call x1, Pallas kernels, local(): pl.pallas_call(functools.partial(kernel, shards, own_blocks, list_width,...  74.3 us
    pallas_call x1, Pallas kernels, local(): pl.pallas_call(hand_over, out_shape=(shape,) * 4, in_specs=[hbm] * 4, out...  2.42 us

profile of v3, /device:TPU:1, one launch (start us, length us, event | category | flops | bytes accessed | tf_op | source)
XLA Modules:
  0.0 77.4 jit_solution(12659633856234904849)
XLA Ops:
  0.6 74.3 %graph_attention.1 = (bf16[256,1024]{1,0:T(8,128)(2,1)}, bf16[256,1024]{1,0:T(8,128)(2,1)}, bf16[256,1024]{1,0:T(8,128)(2,1)}, bf16[256,1024]{1,0:T(8,128)(2,1)}) custom-call(s32[2,8]{1,0:T(2,128)} %nbr_ref.1, s32[2]{0:T(128)} %cnt_ref.1, bf16[256,1024]{1,0:T(8,128)(2,1)} %q_ref.1, bf16[256,1024]{1,0:T(8,128)(2,1)} %k_ref.1, bf16[256,1024]{1,0:T(8,128)(2,1)} %v_ref.1, ...), custom_call_target="tpu_custom_call" | custom-call | tf_op jit(solution)/shard_map/graph_attention/pallas_call | solution.py:314
  74.9 2.4 %hand_over.1 = (bf16[256,1024]{1,0:T(8,128)(2,1)}, bf16[256,1024]{1,0:T(8,128)(2,1)}, bf16[256,1024]{1,0:T(8,128)(2,1)}, bf16[256,1024]{1,0:T(8,128)(2,1)}) custom-call(bf16[256,1024]{1,0:T(8,128)(2,1)} %get-tuple-element.8.refs_0_, bf16[256,1024]{1,0:T(8,128)(2,1)} %get-tuple-element.9.refs_1_, bf16[256,1024]{1,0:T(8,128)(2,1)} %get-tuple-element.10.refs_2_, ...), custom_call_target="tpu_custom_call" | custom-call | tf_op jit(solution)/shard_map/hand_over/pallas_call | solution.py:351

commit v4 on v3

--- a/solution.py
+++ b/solution.py
@@ -10,7 +10,7 @@
 
 HEADS = 16
 LANES = 128
-AHEAD = 3
+AHEAD = 4
 SLOTS = 5
 MASKED = -1e30
 F32 = jnp.float32
@@ -166,17 +166,19 @@
             result[:, columns(c)] = (final + near_r[c, part].astype(F32)).astype(BF16)
 
     def exchange(c):
-        @pl.when(c + AHEAD < chunks)
-        def _():
-            publish(c + AHEAD)
-
-        @pl.when(c + 2 < chunks)
-        def _():
-            pass_on(c + 2)
-
-        @pl.when(c + 1 < chunks)
-        def _():
-            lend_on(c + 1)
+        for extra in range(2):
+            @pl.when(2 * c + extra + AHEAD < chunks)
+            def _():
+                publish(2 * c + extra + AHEAD)
+
+        for extra in range(2):
+            @pl.when(2 * c + extra + 2 < chunks)
+            def _():
+                pass_on(2 * c + extra + 2)
+
+            @pl.when(2 * c + extra + 1 < chunks)
+            def _():
+                lend_on(2 * c + extra + 1)
 
         @pl.when(c >= 1)
         def _():

time: 78.3 us -> 86.8 us (1.11)
  Pallas kernels: 76.7 us -> 85.3 us
    pallas_call x1, Pallas kernels: 74.3 us -> 82.8 us  [local(): pl.pallas_call(functools.partial(kernel, shards, own_blocks, list_width,...]
where the time goes in v4:
time: 86.8 us; the launch traced here: 85.9 us
  Pallas kernels  85.3 us (98%)
    pallas_call x1, Pallas kernels, local(): pl.pallas_call(functools.partial(kernel, shards, own_blocks, list_width,...  82.8 us
    pallas_call x1, Pallas kernels, local(): pl.pallas_call(hand_over, out_shape=(shape,) * 4, in_specs=[hbm] * 4, out...  2.42 us

profile of v4, /device:TPU:1, one launch (start us, length us, event | category | flops | bytes accessed | tf_op | source)
XLA Modules:
  0.0 85.9 jit_solution(5037353365601689019)
XLA Ops:
  0.6 82.8 %graph_attention.1 = (bf16[256,1024]{1,0:T(8,128)(2,1)}, bf16[256,1024]{1,0:T(8,128)(2,1)}, bf16[256,1024]{1,0:T(8,128)(2,1)}, bf16[256,1024]{1,0:T(8,128)(2,1)}) custom-call(s32[2,8]{1,0:T(2,128)} %nbr_ref.1, s32[2]{0:T(128)} %cnt_ref.1, bf16[256,1024]{1,0:T(8,128)(2,1)} %q_ref.1, bf16[256,1024]{1,0:T(8,128)(2,1)} %k_ref.1, bf16[256,1024]{1,0:T(8,128)(2,1)} %v_ref.1, ...), custom_call_target="tpu_custom_call" | custom-call | tf_op jit(solution)/shard_map/graph_attention/pallas_call | solution.py:316
  83.5 2.4 %hand_over.1 = (bf16[256,1024]{1,0:T(8,128)(2,1)}, bf16[256,1024]{1,0:T(8,128)(2,1)}, bf16[256,1024]{1,0:T(8,128)(2,1)}, bf16[256,1024]{1,0:T(8,128)(2,1)}) custom-call(bf16[256,1024]{1,0:T(8,128)(2,1)} %get-tuple-element.8.refs_0_, bf16[256,1024]{1,0:T(8,128)(2,1)} %get-tuple-element.9.refs_1_, bf16[256,1024]{1,0:T(8,128)(2,1)} %get-tuple-element.10.refs_2_, ...), custom_call_target="tpu_custom_call" | custom-call | tf_op jit(solution)/shard_map/hand_over/pallas_call | solution.py:353

commit v5 on v3

--- a/solution.py
+++ b/solution.py
@@ -31,7 +31,7 @@
     out_ref, dq_ref, dk_ref, dv_ref,
     kv, acc, sib_s, sib_r, far_s, far_r, near_s, near_r,
     bias, s_scr, e_scr, d_scr, kt_scr, vt_scr, q_scr, g_scr,
-    q_t, g_t, out_t, dq_t, qs_scr, gs_scr, sends, recvs, loads,
+    q_t, g_t, out_t, dq_t, qs_scr, gs_scr, qp_scr, gp_scr, sum_scr, sends, recvs, loads,
 ):
     rows, width = q_ref.shape
     chunks = width // LANES
@@ -94,6 +94,10 @@
         allowed = jnp.where(entry == key_blk, 1, allowed)
     bias[...] = jnp.where(allowed == 1, 0.0, MASKED).astype(F32)
 
+    for ref in (qp_scr, gp_scr, qs_scr, gs_scr):
+        ref[...] = jnp.zeros(ref.shape, BF16)
+    vt_scr[...] = jnp.ones(vt_scr.shape, BF16)
+
     pl.semaphore_wait(barrier, 4)
 
     def remote(stream, src, dst, c, part, dev):
@@ -190,47 +194,59 @@
         def _():
             close(c - 3)
 
-    def padded(x, h):
-        pieces = []
-        if h:
-            pieces.append(jnp.zeros((h * head_dim, rows), x.dtype))
-        pieces.append(x)
-        if h < pack - 1:
-            pieces.append(jnp.zeros(((pack - 1 - h) * head_dim, rows), x.dtype))
-        return jnp.concatenate(pieces, axis=0)
-
-    def one_head(c, h):
-        head = slice(h * head_dim, (h + 1) * head_dim)
-        here = slice(h * rows, (h + 1) * rows)
-        keys = kv[:, c, 0].reshape(SLOTS * rows, LANES)
-        vals = kv[:, c, 1].reshape(SLOTS * rows, LANES)
-        q_h = q_t[head, :]
-        g_h = g_t[head, :]
-        s_scr[h] = matmul(keys, padded(q_h, h))
-        top = None
-        for r in range(SLOTS * own_blocks):
-            part = jnp.max(s_scr[h, r * blk_len:(r + 1) * blk_len, :], axis=0, keepdims=True)
+    heads = [slice(h * head_dim, (h + 1) * head_dim) for h in range(pack)]
+    lanes = [slice(h * rows, (h + 1) * rows) for h in range(pack)]
+    spans = [slice(slot * rows, (slot + 1) * rows) for slot in range(SLOTS)]
+
+    def score(c, slot, h, state):
+        scores = matmul(kv[slot, c, 0], qp_scr[:, lanes[h]])
+        s_scr[h, spans[slot], :] = scores
+        for b in range(own_blocks):
+            r = slot * own_blocks + b
+            part = jnp.max(scores[b * blk_len:(b + 1) * blk_len], axis=0, keepdims=True)
             part = part + bias[r:r + 1, :]
-            top = part if top is None else jnp.maximum(top, part)
-        total = jnp.zeros((1, rows), F32)
-        for r in range(SLOTS * own_blocks):
+            state["top"] = jnp.maximum(state["top"], part) if slot or b else part
+
+    def weigh(c, slot, h, state):
+        for b in range(own_blocks):
+            r = slot * own_blocks + b
             at = slice(r * blk_len, (r + 1) * blk_len)
-            shift = top - bias[r:r + 1, :]
+            shift = state["top"] - bias[r:r + 1, :]
             e = jnp.exp2((s_scr[h, at, :] - shift) * (factor * math.log2(math.e)))
-            total = total + jnp.sum(e, axis=0, keepdims=True)
-            e_scr[at, here] = e.astype(BF16)
-        mixed = matmul(vt_scr[head, :], e_scr[:, here])
-        inv = 1.0 / total
-        out_h = (mixed * inv).astype(BF16)
-        g_f = g_h.astype(F32)
-        delta = jnp.sum(g_f * out_h.astype(F32), axis=0, keepdims=True)
-        dprobs = matmul(vals, padded(g_h, h))
-        d_scr[:, here] = (e_scr[:, here].astype(F32) * (dprobs - delta)).astype(BF16)
-        dq = matmul(kt_scr[head, :], d_scr[:, here])
-        out_t[head, :] = out_h
-        dq_t[head, :] = (dq * (inv * factor)).astype(BF16)
-        gs_scr[:, here] = padded((g_f * inv).astype(BF16), h)
-        qs_scr[:, here] = padded((q_h.astype(F32) * (inv * factor)).astype(BF16), h)
+            e_scr[at, lanes[h]] = e.astype(BF16)
+        term = matmul(vt_scr[h, :, spans[slot]], e_scr[spans[slot], lanes[h]])
+        state["mixed"] = state["mixed"] + term if slot else term
+
+    def settle(c, h, state):
+        inv = 1.0 / state["mixed"][head_dim:head_dim + 1]
+        out_h = (state["mixed"][:head_dim] * inv).astype(BF16)
+        g_f = g_t[heads[h], :].astype(F32)
+        state["delta"] = jnp.sum(g_f * out_h.astype(F32), axis=0, keepdims=True)
+        state["inv"] = inv
+        out_t[heads[h], :] = out_h
+        gs_scr[heads[h], lanes[h]] = (g_f * inv).astype(BF16)
+        qs_scr[heads[h], lanes[h]] = (q_t[heads[h], :].astype(F32) * (inv * factor)).astype(BF16)
+
+    def reverse(c, slot, h, state):
+        dprobs = matmul(kv[slot, c, 1], gp_scr[:, lanes[h]])
+        d_b = e_scr[spans[slot], lanes[h]] * (dprobs - state["delta"]).astype(BF16)
+        d_scr[spans[slot], lanes[h]] = d_b
+        term = matmul(kt_scr[heads[h], spans[slot]], d_b)
+        state["dq"] = state["dq"] + term if slot else term
+        if slot == SLOTS - 1:
+            dq_t[heads[h], :] = (state["dq"] * (state["inv"] * factor)).astype(BF16)
+
+    def gather(c, slot, h):
+        for part, (left, right) in enumerate(((d_scr, qs_scr), (e_scr, gs_scr))):
+            grad = matmul_nt(left[spans[slot], lanes[h]], right[:, lanes[h]])
+            if h:
+                grad = grad + sum_scr[part, spans[slot], :]
+            if h < pack - 1:
+                sum_scr[part, spans[slot], :] = grad
+            elif slot in (1, 4):
+                sib_s[c, part, slot // 4] = grad.astype(BF16)
+            else:
+                acc[c, max(slot - 1, 0), part] = grad
 
     for c in range(AHEAD):
         publish(c)
@@ -244,25 +260,36 @@
         cols = columns(c)
         q_t[...] = q_scr[:, cols].T
         g_t[...] = g_scr[:, cols].T
+        for h in range(pack):
+            qp_scr[heads[h], lanes[h]] = q_t[heads[h], :]
+            gp_scr[heads[h], lanes[h]] = g_t[heads[h], :]
         for part in range(2):
             to_sibling(c, part).wait_recv()
             lend(c, part).wait_recv()
-        for slot in range(SLOTS):
-            at = slice(slot * rows, (slot + 1) * rows)
-            kt_scr[:, at] = kv[slot, c, 0].T
-            vt_scr[:, at] = kv[slot, c, 1].T
-        for h in range(pack):
-            if h == pack // 2:
+        states = [{} for _ in range(pack)]
+        for step in range(pack + 3):
+            if step == 2:
                 exchange(c)
-            one_head(c, h)
-        for part, (left, right) in enumerate(((d_scr, qs_scr), (e_scr, gs_scr))):
-            grad = matmul_nt(left[...], right[...])
             for slot in range(SLOTS):
-                at = slice(slot * rows, (slot + 1) * rows)
-                if slot in (1, 4):
-                    sib_s[c, part, slot // 4] = grad[at].astype(BF16)
-                else:
-                    acc[c, max(slot - 1, 0), part] = grad[at]
+                if step == 0:
+                    v_t = kv[slot, c, 1].T
+                    for h in range(pack):
+                        vt_scr[h, :head_dim, spans[slot]] = v_t[heads[h]]
+                if step == 1:
+                    kt_scr[:, spans[slot]] = kv[slot, c, 0].T
+                for h in range(pack):
+                    at = step - h
+                    if at == 0:
+                        score(c, slot, h, states[h])
+                    elif at == 1:
+                        weigh(c, slot, h, states[h])
+                    elif at == 2:
+                        if slot == 0:
+                            settle(c, h, states[h])
+                        reverse(c, slot, h, states[h])
+                    elif at == 3:
+                        gather(c, slot, h)
+        for part in range(2):
             grad_sibling(c, part).start()
         out_ref[:, cols] = out_t[...].T
         dq_ref[:, cols] = dq_t[...].T
@@ -330,7 +357,7 @@
             pltpu.VMEM((SLOTS * rows, pack * rows), BF16),
             pltpu.VMEM((SLOTS * rows, pack * rows), BF16),
             pltpu.VMEM((LANES, SLOTS * rows), BF16),
-            pltpu.VMEM((LANES, SLOTS * rows), BF16),
+            pltpu.VMEM((pack, head_dim + 16, SLOTS * rows), BF16),
             pltpu.VMEM((rows, width), BF16),
             pltpu.VMEM((rows, width), BF16),
             pltpu.VMEM((LANES, rows), BF16),
@@ -339,6 +366,9 @@
             pltpu.VMEM((LANES, rows), BF16),
             pltpu.VMEM((LANES, pack * rows), BF16),
             pltpu.VMEM((LANES, pack * rows), BF16),
+            pltpu.VMEM((LANES, pack * rows), BF16),
+            pltpu.VMEM((LANES, pack * rows), BF16),
+            pltpu.VMEM((2, SLOTS * rows, LANES), F32),
             pltpu.SemaphoreType.DMA((7, 2, chunks)),
             pltpu.SemaphoreType.DMA((7, 2, chunks)),
             pltpu.SemaphoreType.DMA((3, chunks)),

time: 78.3 us -> 74.6 us (0.953)
  Pallas kernels: 76.7 us -> 72.9 us
    pallas_call x1, Pallas kernels: 74.3 us -> 70.5 us  [local(): pl.pallas_call(functools.partial(kernel, shards, own_blocks, list_width,...]
where the time goes in v5:
time: 74.6 us; the launch traced here: 73.6 us
  Pallas kernels  72.9 us (98%)
    pallas_call x1, Pallas kernels, local(): pl.pallas_call(functools.partial(kernel, shards, own_blocks, list_width,...  70.5 us
    pallas_call x1, Pallas kernels, local(): pl.pallas_call(hand_over, out_shape=(shape,) * 4, in_specs=[hbm] * 4, out...  2.42 us

profile of v5, /device:TPU:1, one launch (start us, length us, event | category | flops | bytes accessed | tf_op | source)
XLA Modules:
  0.0 73.6 jit_solution(11478668288630376492)
XLA Ops:
  0.6 70.5 %graph_attention.1 = (bf16[256,1024]{1,0:T(8,128)(2,1)}, bf16[256,1024]{1,0:T(8,128)(2,1)}, bf16[256,1024]{1,0:T(8,128)(2,1)}, bf16[256,1024]{1,0:T(8,128)(2,1)}) custom-call(s32[2,8]{1,0:T(2,128)} %nbr_ref.1, s32[2]{0:T(128)} %cnt_ref.1, bf16[256,1024]{1,0:T(8,128)(2,1)} %q_ref.1, bf16[256,1024]{1,0:T(8,128)(2,1)} %k_ref.1, bf16[256,1024]{1,0:T(8,128)(2,1)} %v_ref.1, ...), custom_call_target="tpu_custom_call" | custom-call | tf_op jit(solution)/shard_map/graph_attention/pallas_call | solution.py:341
  71.2 2.4 %hand_over.1 = (bf16[256,1024]{1,0:T(8,128)(2,1)}, bf16[256,1024]{1,0:T(8,128)(2,1)}, bf16[256,1024]{1,0:T(8,128)(2,1)}, bf16[256,1024]{1,0:T(8,128)(2,1)}) custom-call(bf16[256,1024]{1,0:T(8,128)(2,1)} %get-tuple-element.8.refs_0_, bf16[256,1024]{1,0:T(8,128)(2,1)} %get-tuple-element.9.refs_1_, bf16[256,1024]{1,0:T(8,128)(2,1)} %get-tuple-element.10.refs_2_, ...), custom_call_target="tpu_custom_call" | custom-call | tf_op jit(solution)/shard_map/hand_over/pallas_call | solution.py:381

commit v6 on v5

--- a/solution.py
+++ b/solution.py
@@ -134,16 +134,22 @@
     def columns(c):
         return pl.ds(pl.multiple_of(c * LANES, LANES), LANES)
 
+    def publish_part(c, part):
+        load(part, c).wait()
+        to_near(c, part).start()
+        to_sibling(c, part).start()
+
     def publish(c):
         for part in range(2):
-            load(part, c).wait()
-            to_near(c, part).start()
-            to_sibling(c, part).start()
+            publish_part(c, part)
+
+    def pass_part(c, part):
+        to_near(c, part).wait_recv()
+        relay(c, part).start()
 
     def pass_on(c):
         for part in range(2):
-            to_near(c, part).wait_recv()
-            relay(c, part).start()
+            pass_part(c, part)
 
     def lend_on(c):
         for part in range(2):
@@ -248,12 +254,13 @@
             else:
                 acc[c, max(slot - 1, 0), part] = grad
 
-    for c in range(AHEAD):
-        publish(c)
+    publish(0)
+    for c in range(AHEAD - 1):
+        for part in range(2):
+            pass_part(c, part)
+            publish_part(c + 1, part)
     load_q.wait()
     load_g.wait()
-    pass_on(0)
-    pass_on(1)
     lend_on(0)
 
     def body(c, carry):
@@ -314,16 +321,12 @@
 
 
 def hand_over(*refs):
-    sources, results, held, sems = refs[:4], refs[4:8], refs[8], refs[9]
-    reads = [pltpu.make_async_copy(sources[i], held.at[i], sems.at[0, i]) for i in range(4)]
-    writes = [pltpu.make_async_copy(held.at[i], results[i], sems.at[1, i]) for i in range(4)]
-    for read in reads:
-        read.start()
-    for read, write in zip(reads, writes):
-        read.wait()
-        write.start()
-    for write in writes:
-        write.wait()
+    sources, results, sems = refs[:4], refs[4:8], refs[8]
+    copies = [pltpu.make_async_copy(sources[i], results[i], sems.at[i]) for i in range(4)]
+    for copy in copies:
+        copy.start()
+    for copy in copies:
+        copy.wait()
 
 
 def local(shards, query, key_in, value, grad_out, neighbors, counts):
@@ -335,13 +338,18 @@
     tile = (2, rows, LANES)
     vmem = pl.BlockSpec(memory_space=pltpu.VMEM)
     hbm = pl.BlockSpec(memory_space=pl.ANY)
+    fixed = pl.BlockSpec(memory_space=pltpu.HBM)
     smem = pl.BlockSpec(memory_space=pltpu.SMEM)
     shape = jax.ShapeDtypeStruct((rows, width), query.dtype)
     bias_rows = -(-SLOTS * own_blocks // 8) * 8
+    query, key_in, value, grad_out, neighbors, counts = (
+        pltpu.with_memory_space_constraint(x, pltpu.HBM)
+        for x in (query, key_in, value, grad_out, neighbors, counts)
+    )
     results = pl.pallas_call(
         functools.partial(kernel, shards, own_blocks, list_width, head_dim),
         out_shape=(shape,) * 4,
-        in_specs=[smem, smem, hbm, hbm, hbm, hbm],
+        in_specs=[smem, smem, fixed, fixed, fixed, fixed],
         out_specs=(vmem,) * 4,
         scratch_shapes=[
             pltpu.VMEM((SLOTS, chunks) + tile, BF16),
@@ -374,20 +382,19 @@
             pltpu.SemaphoreType.DMA((3, chunks)),
         ],
         compiler_params=pltpu.CompilerParams(
-            collective_id=0, has_side_effects=True, vmem_limit_bytes=56 * 1024 * 1024
+            collective_id=0, has_side_effects=True, vmem_limit_bytes=40 * 1024 * 1024
         ),
         name="graph_attention",
     )(neighbors, counts, query, key_in, value, grad_out)
     return pl.pallas_call(
         hand_over,
         out_shape=(shape,) * 4,
-        in_specs=[hbm] * 4,
-        out_specs=(hbm,) * 4,
+        in_specs=[vmem] * 4,
+        out_specs=(fixed,) * 4,
         scratch_shapes=[
-            pltpu.VMEM((4, rows, width), query.dtype),
-            pltpu.SemaphoreType.DMA((2, 4)),
+            pltpu.SemaphoreType.DMA((4,)),
         ],
-        compiler_params=pltpu.CompilerParams(vmem_limit_bytes=60 * 1024 * 1024),
+        compiler_params=pltpu.CompilerParams(vmem_limit_bytes=16 * 1024 * 1024),
         name="hand_over",
     )(*results)
 

time: 74.6 us -> 72.5 us (0.972)
  Pallas kernels: 72.9 us -> 70.9 us
    pallas_call x1, Pallas kernels: 2.42 us -> 1.35 us  [local(): pl.pallas_call(hand_over, out_shape=(shape,) * 4, in_specs=[vmem] * 4, ou...]
    pallas_call x1, Pallas kernels: 70.5 us -> 69.5 us  [local(): pl.pallas_call(functools.partial(kernel, shards, own_blocks, list_width,...]
where the time goes in v6:
time: 72.5 us; the launch traced here: 71.5 us
  Pallas kernels  70.9 us (98%)
    pallas_call x1, Pallas kernels, local(): pl.pallas_call(functools.partial(kernel, shards, own_blocks, list_width,...  69.5 us

profile of v6, /device:TPU:1, one launch (start us, length us, event | category | flops | bytes accessed | tf_op | source)
XLA Modules:
  0.0 71.5 jit_solution(4789918277102946189)
XLA Ops:
  0.6 69.5 %graph_attention.1 = (bf16[256,1024]{1,0:T(8,128)(2,1)S(1)}, bf16[256,1024]{1,0:T(8,128)(2,1)S(1)}, bf16[256,1024]{1,0:T(8,128)(2,1)S(1)}, bf16[256,1024]{1,0:T(8,128)(2,1)S(1)}) custom-call(s32[2,8]{1,0:T(2,128)} %nbr_ref.1, s32[2]{0:T(128)} %cnt_ref.1, bf16[256,1024]{1,0:T(8,128)(2,1)} %q_ref.1, bf16[256,1024]{1,0:T(8,128)(2,1)} %k_ref.1, ...), custom_call_target="tpu_custom_call" | custom-call | tf_op jit(solution)/shard_map/graph_attention/pallas_call | solution.py:349
  70.2 1.3 %hand_over.1 = (bf16[256,1024]{1,0:T(8,128)(2,1)}, bf16[256,1024]{1,0:T(8,128)(2,1)}, bf16[256,1024]{1,0:T(8,128)(2,1)}, bf16[256,1024]{1,0:T(8,128)(2,1)}) custom-call(bf16[256,1024]{1,0:T(8,128)(2,1)S(1)} %get-tuple-element.8.refs_0_, bf16[256,1024]{1,0:T(8,128)(2,1)S(1)} %get-tuple-element.9.refs_1_, bf16[256,1024]{1,0:T(8,128)(2,1)S(1)} %get-tuple-element.10.refs_2_, ...), custom_call_target="tpu_custom_call" | custom-call | tf_op jit(solution)/shard_map/hand_over/pallas_call | solution.py:389

commit v7 on v6

--- a/solution.py
+++ b/solution.py
@@ -180,6 +180,14 @@
         def _():
             publish(c + AHEAD)
 
+        @pl.when(c >= 1)
+        def _():
+            send_far(c - 1)
+
+        @pl.when(c >= 2)
+        def _():
+            send_near(c - 2)
+
         @pl.when(c + 2 < chunks)
         def _():
             pass_on(c + 2)
@@ -187,14 +195,6 @@
         @pl.when(c + 1 < chunks)
         def _():
             lend_on(c + 1)
-
-        @pl.when(c >= 1)
-        def _():
-            send_far(c - 1)
-
-        @pl.when(c >= 2)
-        def _():
-            send_near(c - 2)
 
         @pl.when(c >= 3)
         def _():
@@ -277,7 +277,7 @@
         for step in range(pack + 3):
             if step == 2:
                 exchange(c)
-            for slot in range(SLOTS):
+            for slot in (1, 4, 0, 2, 3) if step == pack + 2 else range(SLOTS):
                 if step == 0:
                     v_t = kv[slot, c, 1].T
                     for h in range(pack):
@@ -296,8 +296,9 @@
                         reverse(c, slot, h, states[h])
                     elif at == 3:
                         gather(c, slot, h)
-        for part in range(2):
-            grad_sibling(c, part).start()
+                if step == pack + 2 and slot == 4:
+                    for part in range(2):
+                        grad_sibling(c, part).start()
         out_ref[:, cols] = out_t[...].T
         dq_ref[:, cols] = dq_t[...].T
         return carry

time: 72.5 us -> 74.1 us (1.022)
  Pallas kernels: 70.9 us -> 72.4 us
    pallas_call x1, Pallas kernels: 69.5 us -> 71.1 us  [local(): pl.pallas_call(functools.partial(kernel, shards, own_blocks, list_width,...]
where the time goes in v7:
time: 74.1 us; the launch traced here: 73.1 us
  Pallas kernels  72.4 us (98%)
    pallas_call x1, Pallas kernels, local(): pl.pallas_call(functools.partial(kernel, shards, own_blocks, list_width,...  71.1 us

profile of v7, /device:TPU:1, one launch (start us, length us, event | category | flops | bytes accessed | tf_op | source)
XLA Modules:
  0.0 73.1 jit_solution(18214931427227248506)
XLA Ops:
  0.6 71.1 %graph_attention.1 = (bf16[256,1024]{1,0:T(8,128)(2,1)S(1)}, bf16[256,1024]{1,0:T(8,128)(2,1)S(1)}, bf16[256,1024]{1,0:T(8,128)(2,1)S(1)}, bf16[256,1024]{1,0:T(8,128)(2,1)S(1)}) custom-call(s32[2,8]{1,0:T(2,128)} %nbr_ref.1, s32[2]{0:T(128)} %cnt_ref.1, bf16[256,1024]{1,0:T(8,128)(2,1)} %q_ref.1, bf16[256,1024]{1,0:T(8,128)(2,1)} %k_ref.1, ...), custom_call_target="tpu_custom_call" | custom-call | tf_op jit(solution)/shard_map/graph_attention/pallas_call | solution.py:350
  71.7 1.3 %hand_over.1 = (bf16[256,1024]{1,0:T(8,128)(2,1)}, bf16[256,1024]{1,0:T(8,128)(2,1)}, bf16[256,1024]{1,0:T(8,128)(2,1)}, bf16[256,1024]{1,0:T(8,128)(2,1)}) custom-call(bf16[256,1024]{1,0:T(8,128)(2,1)S(1)} %get-tuple-element.8.refs_0_, bf16[256,1024]{1,0:T(8,128)(2,1)S(1)} %get-tuple-element.9.refs_1_, bf16[256,1024]{1,0:T(8,128)(2,1)S(1)} %get-tuple-element.10.refs_2_, ...), custom_call_target="tpu_custom_call" | custom-call | tf_op jit(solution)/shard_map/hand_over/pallas_call | solution.py:390

commit v8 on v6

--- a/solution.py
+++ b/solution.py
@@ -188,6 +188,7 @@
         def _():
             lend_on(c + 1)
 
+    def exchange_grads(c):
         @pl.when(c >= 1)
         def _():
             send_far(c - 1)
@@ -275,8 +276,10 @@
             lend(c, part).wait_recv()
         states = [{} for _ in range(pack)]
         for step in range(pack + 3):
-            if step == 2:
+            if step == 1:
                 exchange(c)
+            if step == 3:
+                exchange_grads(c)
             for slot in range(SLOTS):
                 if step == 0:
                     v_t = kv[slot, c, 1].T

time: 72.5 us -> 72.6 us (level)
  no operation moved by 1% of the time
where the time goes in v8:
time: 72.6 us; the launch traced here: 71.8 us
  Pallas kernels  71.2 us (98%)
    pallas_call x1, Pallas kernels, local(): pl.pallas_call(functools.partial(kernel, shards, own_blocks, list_width,...  69.8 us

profile of v8, /device:TPU:1, one launch (start us, length us, event | category | flops | bytes accessed | tf_op | source)
XLA Modules:
  0.0 71.8 jit_solution(12180635434466228543)
XLA Ops:
  0.6 69.8 %graph_attention.1 = (bf16[256,1024]{1,0:T(8,128)(2,1)S(1)}, bf16[256,1024]{1,0:T(8,128)(2,1)S(1)}, bf16[256,1024]{1,0:T(8,128)(2,1)S(1)}, bf16[256,1024]{1,0:T(8,128)(2,1)S(1)}) custom-call(s32[2,8]{1,0:T(2,128)} %nbr_ref.1, s32[2]{0:T(128)} %cnt_ref.1, bf16[256,1024]{1,0:T(8,128)(2,1)} %q_ref.1, bf16[256,1024]{1,0:T(8,128)(2,1)} %k_ref.1, ...), custom_call_target="tpu_custom_call" | custom-call | tf_op jit(solution)/shard_map/graph_attention/pallas_call | solution.py:352
  70.5 1.3 %hand_over.1 = (bf16[256,1024]{1,0:T(8,128)(2,1)}, bf16[256,1024]{1,0:T(8,128)(2,1)}, bf16[256,1024]{1,0:T(8,128)(2,1)}, bf16[256,1024]{1,0:T(8,128)(2,1)}) custom-call(bf16[256,1024]{1,0:T(8,128)(2,1)S(1)} %get-tuple-element.8.refs_0_, bf16[256,1024]{1,0:T(8,128)(2,1)S(1)} %get-tuple-element.9.refs_1_, bf16[256,1024]{1,0:T(8,128)(2,1)S(1)} %get-tuple-element.10.refs_2_, ...), custom_call_target="tpu_custom_call" | custom-call | tf_op jit(solution)/shard_map/hand_over/pallas_call | solution.py:392
